TPU v7x, 256 devices: a whole 4x4x8 slice. The times are simulated.
256 devices in a mesh: depth: 2 (over core), row: 8 (over z), col: 16 (over y, x).
Axes of the slice: x: 4, y: 4, z: 8, core: 2. Of those that a mesh axis runs over, the one named last changes fastest.
Arguments:
- tokens: bfloat16 [2048, 6144], P(('depth', 'row'), 'col'), may hold values from -6 to 6
- weight: bfloat16 [6144, 24576], P('col', 'row'), may hold values from -0.078125 to 0.078125
- cotangent: bfloat16 [2048, 24576], P(('depth', 'col'), 'row'), may hold values from -6 to 6
Outputs:
- activated: bfloat16 [2048, 24576], P(('depth', 'col'), 'row')
- grad_tokens: bfloat16 [2048, 6144], P(('depth', 'row'), 'col')
- grad_weight: bfloat16 [6144, 24576], P('col', 'row')
All inputs are finite; a program needn't handle non-finite values.
Results may differ from a plain program's by a relative error of at most 0.022.
Values may be sent and summed in bfloat16 or wider, within the bound.
A program may use at most 128 MiB of HBM per device.

v0:
```python
import math

import jax
import jax.numpy as jnp
from jax import lax
from jax.sharding import PartitionSpec as P


def gelu_parts(hidden):
    cdf = 0.5 * (1.0 + jax.scipy.special.erf(hidden * (1.0 / math.sqrt(2.0))))
    density = jnp.exp(-0.5 * hidden * hidden) * (1.0 / math.sqrt(2.0 * math.pi))
    return (cdf, density)


def local(tokens, weight, cotangent):
    panel = lax.all_gather(tokens, "row", axis=0, tiled=True)
    rows = panel
    hidden = lax.psum_scatter(
        jnp.dot(rows, weight, preferred_element_type=jnp.float32).astype(jnp.bfloat16),
        "col",
        scatter_dimension=0,
        tiled=True,
    ).astype(jnp.float32)
    cdf, density = gelu_parts(hidden)
    activated = (hidden * cdf).astype(jnp.bfloat16)
    grad_hidden = (cotangent.astype(jnp.float32) * (cdf + hidden * density)).astype(jnp.bfloat16)
    grad_panel = lax.all_gather(grad_hidden, "col", axis=0, tiled=True)
    rows = grad_panel
    grad_tokens = lax.psum_scatter(
        lax.dot_general(
            rows, weight, (((1,), (1,)), ((), ())), preferred_element_type=jnp.float32
        ).astype(jnp.bfloat16),
        "row",
        scatter_dimension=0,
        tiled=True,
    )
    partial_weight = lax.dot_general(
        panel, grad_panel, (((0,), (0,)), ((), ())), preferred_element_type=jnp.float32
    )
    grad_weight = lax.psum(partial_weight.astype(jnp.bfloat16), "depth")
    return (activated, grad_tokens, grad_weight)


def solution(mesh):
    placed = (P(("depth", "row"), "col"), P("col", "row"), P(("depth", "col"), "row"))
    return jax.shard_map(
        local,
        mesh=mesh,
        in_specs=placed,
        out_specs=(P(("depth", "col"), "row"), P(("depth", "row"), "col"), P("col", "row")),
        check_vma=False,
    )
```

profile of v0, /device:TPU:4, one launch (start us, length us, event | category | flops | bytes accessed | tf_op | source)
XLA Modules:
  0.0 286.4 jit_solution(6347303136628829402)
XLA Ops:
  7.2 0.0 copy-start
  7.2 0.0 reduce-scatter.3.cloned.1.call-start
  7.2 30.2 %all_gather.6 = bf16[1024,384]{1,0:T(8,128)(2,1)S(1)} all-gather(bf16[128,384]{1,0:T(8,128)(2,1)} %param.3), channel_id=1, replica_groups=mesh['depth'=2,'row'=8,'col'=16] {'row'}, dimensions={0}, use_global_device_ids=true | all-gather | bytes 884736 | tf_op jit(solution)/shard_map/all_gather | solution.py:16
  37.4 0.0 copy-done
  37.4 5.4 %convolution_convert_fusion = bf16[1024,3072]{1,0:T(8,128)(2,1)} fusion(bf16[1024,384]{1,0:T(8,128)(2,1)S(1)} %all_gather.6, bf16[384,3072]{1,0:T(8,128)(2,1)S(1)} %copy-done), kind=kOutput, calls=%fused_computation | convolution fusion | flops 2419064832 | bytes 9437184 | tf_op jit(solution)/shard_map/dot_general | solution.py:19
  42.8 0.0 copy-start.1
  42.8 0.0 reduce-scatter.3.cloned.1.call-update
  42.8 0.0 all-gather.2.cloned.1.call-start
  42.9 85.5 %reduce-scatter.3.cloned.1.call-done = bf16[64,3072]{1,0:T(8,128)(2,1)} async-done(((bf16[1024,3072]{1,0:T(8,128)(2,1)}), bf16[64,3072]{1,0:T(8,128)(2,1)}) %reduce-scatter.3.cloned.1.call-update) | async-done | bytes 393232 | tf_op jit(solution)/shard_map/reduce_scatter | solution.py:18
  128.4 0.0 copy-done.1
  128.4 2.3 fusion.9
  130.6 0.0 all-gather.2.cloned.1.call-update
  130.7 0.0 all-reduce.2.cloned.1.call-start
  130.7 66.8 %all-gather.2.cloned.1.call-done = bf16[1024,3072]{1,0:T(8,128)(2,1)} async-done(((bf16[64,3072]{1,0:T(8,128)(2,1)}), bf16[1024,3072]{1,0:T(8,128)(2,1)}) %all-gather.2.cloned.1.call-update) | async-done | bytes 6291472 | tf_op jit(solution)/shard_map/all_gather | solution.py:27
  197.5 7.7 %fusion = bf16[384,3072]{0,1:T(8,128)(2,1)} fusion(bf16[1024,3072]{1,0:T(8,128)(2,1)} %all-gather.2.cloned.1.call-done, bf16[1024,384]{1,0:T(8,128)(2,1)S(1)} %all_gather.6), kind=kOutput, calls=%fused_computation.2 | convolution fusion | flops 2417098752 | bytes 9437184 | tf_op jit(solution)/shard_map/dot_general | solution.py:37
  205.2 0.0 all-reduce.2.cloned.1.call-update
  205.2 0.0 reduce-scatter.5.cloned.1.call-start
  205.3 6.6 %convolution_convert_fusion.2 = bf16[1024,384]{1,0:T(8,128)(2,1)} fusion(bf16[1024,3072]{1,0:T(8,128)(2,1)} %all-gather.2.cloned.1.call-done, bf16[384,3072]{1,0:T(8,128)(2,1)S(1)} %copy-done), kind=kOutput, calls=%fused_computation.8 | convolution fusion | flops 2416312320 | bytes 9437184 | tf_op jit(solution)/shard_map/dot_general | solution.py:30
  211.9 0.0 reduce-scatter.5.cloned.1.call-update
  211.9 25.7 %all-reduce.2.cloned.1.call-done = bf16[384,3072]{0,1:T(8,128)(2,1)} async-done(((bf16[384,3072]{0,1:T(8,128)(2,1)}), bf16[384,3072]{0,1:T(8,128)(2,1)}) %all-reduce.2.cloned.1.call-update) | async-done | bytes 2359312 | tf_op jit(solution)/shard_map/psum | solution.py:40
  237.5 4.3 %copy.6 = bf16[384,3072]{1,0:T(8,128)(2,1)} copy(bf16[384,3072]{0,1:T(8,128)(2,1)} %all-reduce.2.cloned.1.call-done) | data formatting | bytes 4718592
  241.8 38.0 %reduce-scatter.5.cloned.1.call-done = bf16[128,384]{1,0:T(8,128)(2,1)} async-done(((bf16[1024,384]{1,0:T(8,128)(2,1)}), bf16[128,384]{1,0:T(8,128)(2,1)}) %reduce-scatter.5.cloned.1.call-update) | async-done | bytes 98320 | tf_op jit(solution)/shard_map/reduce_scatter | solution.py:29
Async XLA Ops:
  7.2 30.2 %copy-start = (bf16[384,3072]{1,0:T(8,128)(2,1)S(1)}, bf16[384,3072]{1,0:T(8,128)(2,1)}, u32[]{:S(2)}) copy-start(bf16[384,3072]{1,0:T(8,128)(2,1)} %param.4) | copy-start | bytes 7077892
  7.2 121.2 %reduce-scatter.3.cloned.1.call-start = ((), (), s32[]{:S(2)}) async-start(), calls=%async_computation.2 | async-start | bytes 6684672 | tf_op jit(solution)/shard_map/reduce_scatter | solution.py:18
  42.8 85.6 %copy-start.1 = (bf16[64,3072]{1,0:T(8,128)(2,1)S(1)}, bf16[64,3072]{1,0:T(8,128)(2,1)}, u32[]{:S(2)}) copy-start(bf16[64,3072]{1,0:T(8,128)(2,1)} %param.5) | copy-start | bytes 1179652
  42.8 154.7 %all-gather.2.cloned.1.call-start = ((), (), s32[]{:S(2)}) async-start(), calls=%async_computation.3 | async-start | bytes 6684672 | tf_op jit(solution)/shard_map/all_gather | solution.py:27
  130.7 106.9 %all-reduce.2.cloned.1.call-start = ((), (), s32[]{:S(2)}) async-start(), calls=%async_computation.5 | async-start | bytes 4718592 | tf_op jit(solution)/shard_map/psum | solution.py:40
  205.2 74.6 %reduce-scatter.5.cloned.1.call-start = ((), (), s32[]{:S(2)}) async-start(), calls=%async_computation.4 | async-start | bytes 884736 | tf_op jit(solution)/shard_map/reduce_scatter | solution.py:29
Sparse Core Ops, SparseCore 0:
  43.0 85.3 reduce-scatter.2
  131.4 66.1 all-gather.1
  205.4 32.1 all-reduce.1
  240.7 39.1 reduce-scatter.4
where the time goes:
time: 287 us; the launch traced here: 286 us
  waiting for transfers between devices  216 us (75%)
  blocking collectives  30.2 us (11%)
  matrix products  19.7 us (7%)
  between operations  13.8 us (5%)
  local copies, waits for them, and re-layouts  4.28 us (1%)
    reduce_scatter x1, waiting for transfers between devices, local(): lax.psum_scatter(jnp.dot(rows, weight, preferred_element_type=jnp.float32...  85.5 us
    all_gather x1, waiting for transfers between devices, local(): grad_panel = lax.all_gather(grad_hidden, 'col', axis=0, tiled=True)  66.8 us
    reduce_scatter x1, waiting for transfers between devices, local(): lax.psum_scatter(lax.dot_general(rows, weight, (((1,), (1,)), ((), ())),...  38 us
    all_gather x1, blocking collectives, local(): panel = lax.all_gather(tokens, 'row', axis=0, tiled=True)  30.2 us
    psum x1, waiting for transfers between devices, local(): grad_weight = lax.psum(partial_weight.astype(jnp.bfloat16), 'depth')  25.7 us
    dot_general x1, matrix products, local(): lax.dot_general(panel, grad_panel, (((0,), (0,)), ((), ())), preferred_el...  7.66 us
    dot_general x1, matrix products, local(): lax.dot_general(rows, weight, (((1,), (1,)), ((), ())), preferred_element...  6.57 us
  transfers between devices with their start and end apart: 4, of which 4 were waited for; matrix products, arithmetic and copies ran while one was open for 4% of the time, Pallas kernels for 0%

commit v1 on v0

v1 whole, which is shorter than its diff:
```python
import functools
import math

import jax
import jax.numpy as jnp
from jax import lax
from jax.experimental import pallas as pl
from jax.experimental.pallas import tpu as pltpu
from jax.sharding import PartitionSpec as P

MESH = pl.DeviceIdType.MESH
NCH = 2
SIDE = 4
ROWS = 8
BF16 = jnp.bfloat16
F32 = jnp.float32


def gelu_parts(hidden):
    cdf = 0.5 * (1.0 + lax.erf(hidden * (1.0 / math.sqrt(2.0))))
    density = jnp.exp(-0.5 * hidden * hidden) * (1.0 / math.sqrt(2.0 * math.pi))
    return (cdf, density)


def schedule():
    tasks = [("I", 0, j) for j in (2, 1, 3, 0)]
    for n in range(NCH):
        more = n + 1 < NCH
        tasks += [("F", n, 2), ("F", n, 1), ("D", n, 2), ("F", n, 3), ("D", n, 1), ("F", n, 0)]
        if more:
            tasks += [("I", n + 1, 2), ("D", n, 3), ("I", n + 1, 1), ("D", n, 0)]
            tasks += [("I", n + 1, 3), ("F2", n, 0), ("I", n + 1, 0), ("D2", n, 0)]
        else:
            tasks += [("D", n, 3), ("D", n, 0), ("F2", n, 0), ("D2", n, 0)]
    for n in range(NCH):
        tasks += [("B", n, 0), ("A1", n, 0), ("B", n, 1), ("B", n, 3), ("A2", n, 0), ("C", n, 0)]
        tasks += [("B", n, 2), ("C", n, 1), ("C", n, 3), ("C", n, 2)]
    return tasks


def kernel(
    tok_hbm, w_hbm, cot_hbm, act_hbm, own_hbm, other_hbm, gt_hbm,
    w, cot, act, tok, tok_t, part, f1, r1, s, f2, r2, g, gw, gwb, gt, zsend, zrecv,
    local_sem, out_sem, z_send, z_recv, send, f1_sem, r1_sem, f2_sem, r2_sem, g_sem,
    dep_send, dep_recv, zs_send, zs_recv,
):
    fh = part.shape[-1]
    half = 32
    depth, row, col = (lax.axis_index(a) for a in ("depth", "row", "col"))
    yx = (col // SIDE, col % SIDE)
    lo, hi = pl.ds(0, half), pl.ds(half, half)

    loads = [
        pltpu.make_async_copy(tok_hbm, tok.at[0, pl.ds(2 * row, 2)], local_sem.at[0]),
        pltpu.make_async_copy(w_hbm, w, local_sem.at[1]),
        pltpu.make_async_copy(cot_hbm, cot, local_sem.at[2]),
    ]
    for load in loads:
        load.start()

    def grid_device(axis, delta):
        at = list(yx)
        at[axis] = (at[axis] + delta + SIDE) % SIDE
        return {"col": at[0] * SIDE + at[1]}

    def row_device(delta):
        return {"row": (row + delta + ROWS) % ROWS}

    other = {"depth": 1 - depth}

    barrier = pltpu.get_barrier_semaphore()
    peers = [row_device(d) for d in range(1, ROWS)]
    peers += [grid_device(axis, delta) for axis in (0, 1) for delta in (1, -1)]
    peers += [other]
    for peer in peers:
        pl.semaphore_signal(barrier, inc=1, device_id=peer, device_id_type=MESH)
    pl.semaphore_wait(barrier, len(peers))

    def remote(src, dst, ssem, rsem, device):
        return pltpu.make_async_remote_copy(
            src_ref=src, dst_ref=dst, send_sem=ssem, recv_sem=rsem,
            device_id=device, device_id_type=MESH,
        )

    def push(src, dst, ssem, rsem, device):
        remote(src, dst, ssem, rsem, device).start()

    def arrived(ref, rsem):
        remote(ref, ref, send.at[0, 0, 0], rsem, other).wait_recv()

    def sent(ref, ssem):
        remote(ref, ref, ssem, f2_sem.at[0, 0], other).wait_send()

    def rows_of(delta):
        return 2 * ((row + delta + ROWS) % ROWS)

    def two(delta):
        return tok.at[0, pl.ds(rows_of(delta), 2)]

    gt[...] = jnp.zeros_like(gt)
    loads[0].wait()
    push(two(0), two(0), z_send.at[0], z_recv.at[0], row_device(1))
    push(two(0), two(0), z_send.at[1], z_recv.at[1], row_device(-1))
    for step in (1, 2, 3):
        arrived(two(-step), z_recv.at[2 * step - 2])
        if step < 3:
            src = two(-step)
        else:
            src = tok.at[0, rows_of(-step)]
        push(src, src, z_send.at[2 * step], z_recv.at[2 * step if step < 3 else 6], row_device(1))
        arrived(two(step), z_recv.at[2 * step - 1])
        if step < 3:
            src = two(step)
        else:
            src = tok.at[0, rows_of(step) + 1]
        push(src, src, z_send.at[2 * step + 1], z_recv.at[2 * step + 1 if step < 3 else 7], row_device(-1))
    arrived(tok.at[0, rows_of(4)], z_recv.at[6])
    arrived(tok.at[0, rows_of(4) + 1], z_recv.at[7])
    for at_y in range(SIDE):
        for at_x in range(SIDE):
            tok[1, at_x * SIDE + at_y] = tok[0, at_y * SIDE + at_x]
    loads[1].wait()

    def transposes():
        for h in range(2):
            for at in range(SIDE):
                tok_t[h, at] = tok[h, pl.ds(SIDE * at, SIDE)].reshape(256, 384).T

    def ring(h):
        axis_a, axis_b = (1, 0) if h == 0 else (0, 1)
        return axis_a, axis_b, yx[axis_a], yx[axis_b]

    def slot(h, j, i):
        _, _, a, b = ring(h)
        return ((b + j) % SIDE) * SIDE + (a + i) % SIDE

    def columns(n, h):
        return pl.ds((2 * n + h) * fh, fh)

    def group(h, j):
        _, _, _, b = ring(h)
        return (b + j) % SIDE

    def task_i(n, h, j):
        axis_a = ring(h)[0]
        four = pl.ds(SIDE * group(h, j), SIDE)
        x = tok[h, four].reshape(256, 384)
        y = jnp.dot(x, w[:, columns(n, h)], preferred_element_type=F32).astype(BF16)
        part[n, h, four] = y.reshape(SIDE, 64, fh)
        right, left = grid_device(axis_a, 1), grid_device(axis_a, -1)
        ssem = send.at[n, h, 0]
        far = part.at[n, h, slot(h, j, 2)]
        push(far.at[lo], f1.at[n, h, j, 0], ssem, f1_sem.at[n, h, j], right)
        push(far.at[hi], f1.at[n, h, j, 1], ssem, f1_sem.at[n, h, j], left)
        push(part.at[n, h, slot(h, j, 1), hi], r1.at[n, h, j, 0, hi], ssem, r1_sem.at[n, h, j], right)
        push(part.at[n, h, slot(h, j, 3), lo], r1.at[n, h, j, 1, lo], ssem, r1_sem.at[n, h, j], left)

    def task_f(n, h, j):
        axis_a = ring(h)[0]
        right, left = grid_device(axis_a, 1), grid_device(axis_a, -1)
        ssem = send.at[n, h, 1]
        arrived(f1.at[n, h, j], f1_sem.at[n, h, j])
        f1[n, h, j, 0] = (f1[n, h, j, 0].astype(F32) + part[n, h, slot(h, j, 1), lo].astype(F32)).astype(BF16)
        push(f1.at[n, h, j, 0], r1.at[n, h, j, 0, lo], ssem, r1_sem.at[n, h, j], right)
        f1[n, h, j, 1] = (f1[n, h, j, 1].astype(F32) + part[n, h, slot(h, j, 3), hi].astype(F32)).astype(BF16)
        push(f1.at[n, h, j, 1], r1.at[n, h, j, 1, hi], ssem, r1_sem.at[n, h, j], left)

    def task_d(n, h, j):
        axis_b = ring(h)[1]
        right, left = grid_device(axis_b, 1), grid_device(axis_b, -1)
        ssem = send.at[n, h, 2]
        arrived(r1.at[n, h, j], r1_sem.at[n, h, j])
        total = part[n, h, slot(h, j, 0)].astype(F32)
        total = total + r1[n, h, j, 0].astype(F32) + r1[n, h, j, 1].astype(F32)
        s[n, h, j] = total.astype(BF16)
        if j == 2:
            push(s.at[n, h, 2, lo], f2.at[n, h, 0], ssem, f2_sem.at[n, h], right)
            push(s.at[n, h, 2, hi], f2.at[n, h, 1], ssem, f2_sem.at[n, h], left)
        elif j == 1:
            push(s.at[n, h, 1, hi], r2.at[n, h, 0, hi], ssem, r2_sem.at[n, h], right)
        elif j == 3:
            push(s.at[n, h, 3, lo], r2.at[n, h, 1, lo], ssem, r2_sem.at[n, h], left)

    def task_f2(n, h):
        axis_b = ring(h)[1]
        right, left = grid_device(axis_b, 1), grid_device(axis_b, -1)
        ssem = send.at[n, h, 2]
        arrived(f2.at[n, h], f2_sem.at[n, h])
        f2[n, h, 0] = (f2[n, h, 0].astype(F32) + s[n, h, 1, lo].astype(F32)).astype(BF16)
        push(f2.at[n, h, 0], r2.at[n, h, 0, lo], ssem, r2_sem.at[n, h], right)
        f2[n, h, 1] = (f2[n, h, 1].astype(F32) + s[n, h, 3, hi].astype(F32)).astype(BF16)
        push(f2.at[n, h, 1], r2.at[n, h, 1, hi], ssem, r2_sem.at[n, h], left)

    def share(n, h, j, i, axis, delta):
        axis_a = ring(h)[0]
        nj, ni = (j, (i - delta) % SIDE) if axis == axis_a else ((j - delta) % SIDE, i)
        far = 2 in (ni if axis == axis_a else nj,)
        block = g.at[n, h, slot(h, j, i)]
        if far:
            block = block.at[lo if delta == 1 else hi]
        push(block, block, send.at[n, h, 3], g_sem.at[n, h, nj, ni], grid_device(axis, delta))

    def task_d2(n, h):
        axis_a, axis_b, _, _ = ring(h)
        arrived(r2.at[n, h], r2_sem.at[n, h])
        mine = slot(h, 0, 0)

        @pl.loop(0, 4)
        def _(at):
            rows = pl.ds(pl.multiple_of(at * 16, 16), 16)
            hidden = s[n, h, 0, rows].astype(F32) + r2[n, h, 0, rows].astype(F32) + r2[n, h, 1, rows].astype(F32)
            cdf, density = gelu_parts(hidden)
            act[rows, columns(n, h)] = (hidden * cdf).astype(BF16)
            grad = cot[rows, columns(n, h)].astype(F32) * (cdf + hidden * density)
            g[n, h, mine, rows] = grad.astype(BF16)

        for axis in (axis_b, axis_a):
            for delta in (1, -1):
                share(n, h, 0, 0, axis, delta)

    def block_here(n, h, j, i):
        arrived(g.at[n, h, slot(h, j, i)], g_sem.at[n, h, j, i])

    def task_b(n, h, j):
        axis_a = ring(h)[0]
        block_here(n, h, j, 3)
        share(n, h, j, 3, axis_a, 1)
        block_here(n, h, j, 1)
        share(n, h, j, 1, axis_a, -1)

    def task_a1(n, h):
        axis_a, axis_b, _, _ = ring(h)
        for j, delta in ((3, 1), (1, -1)):
            block_here(n, h, j, 0)
            share(n, h, j, 0, axis_b, delta)
            share(n, h, j, 0, axis_a, 1)
            share(n, h, j, 0, axis_a, -1)

    def task_a2(n, h):
        axis_a = ring(h)[0]
        block_here(n, h, 2, 0)
        share(n, h, 2, 0, axis_a, 1)
        share(n, h, 2, 0, axis_a, -1)

    finished = (set(), set())
    pushed = set()

    def task_c(n, h, j, last):
        block_here(n, h, j, 2)
        at = group(h, j)
        rows = g[n, h, pl.ds(SIDE * at, SIDE)].reshape(256, fh)
        delta_t = lax.dot_general(
            rows, w[:, columns(n, h)], (((1,), (1,)), ((), ())), preferred_element_type=F32
        )
        if h == 0:
            four = pl.ds(SIDE * at, SIDE)
            delta_t = delta_t.reshape(SIDE, 64, 384)
            gt[four] = gt[four] + delta_t
        else:
            for at_y in range(SIDE):
                piece = delta_t[64 * at_y : 64 * at_y + 64]
                gt[SIDE * at_y + at] = gt[SIDE * at_y + at] + piece
        if n == NCH - 1:
            finished[h].add(j)
            for jy in finished[0]:
                for ix in finished[1]:
                    if (jy, ix) not in pushed:
                        pushed.add((jy, ix))
                        send_tokens(jy, ix)
        delta_w = jnp.dot(tok_t[h, at], rows, preferred_element_type=F32)
        if j == 0:
            gw[h] = delta_w
        elif not last:
            gw[h] = gw[h] + delta_w
        else:
            gwb[n, h] = (gw[h] + delta_w).astype(BF16)
            cols = columns(n, h)
            push(gwb.at[n, h], other_hbm.at[:, cols], dep_send.at[n, h], dep_recv.at[n, h], other)
            pltpu.make_async_copy(gwb.at[n, h], own_hbm.at[:, cols], out_sem.at[n, h]).start()

    def send_tokens(jy, ix):
        at = ((yx[0] + jy) % SIDE) * SIDE + (yx[1] + ix) % SIDE
        zsend[at] = gt[at].astype(BF16)
        to = at // 2
        ahead = (to - row + ROWS) % ROWS

        @pl.when(ahead != 0)
        def _():
            place = ROWS - 1 - ahead
            push(zsend.at[at], zrecv.at[place, at % 2], zs_send.at[0], zs_recv.at[0], {"row": to})

    cot_waited = False
    done_transposes = False
    for name, n, j in schedule():
        if name == "D2" and not cot_waited:
            loads[2].wait()
            cot_waited = True
        if name == "I":
            for h in (0, 1):
                task_i(n, h, j)
            if not done_transposes and j == 0:
                transposes()
                done_transposes = True
        for h in (0, 1):
            if name == "F":
                task_f(n, h, j)
            elif name == "D":
                task_d(n, h, j)
            elif name == "F2":
                task_f2(n, h)
            elif name == "D2":
                task_d2(n, h)
            elif name == "B":
                task_b(n, h, j)
            elif name == "A1":
                task_a1(n, h)
            elif name == "A2":
                task_a2(n, h)
            elif name == "C":
                task_c(n, h, j, j == 2)

    act_out = pltpu.make_async_copy(act, act_hbm, local_sem.at[0])
    act_out.start()
    arrived(zrecv, zs_recv.at[0])
    for at in range(2):
        total = gt[2 * row + at].astype(BF16).astype(F32)
        for place in range(ROWS - 1):
            total = total + zrecv[place, at].astype(F32)
        zsend[2 * row + at] = total.astype(BF16)
    gt_out = pltpu.make_async_copy(zsend.at[pl.ds(2 * row, 2)], gt_hbm, local_sem.at[1])
    gt_out.start()

    for n in range(NCH):
        for h in (0, 1):
            sent(r1.at[n, h], send.at[n, h, 0])
            sent(s.at[n, h], send.at[n, h, 1])
            sent(s.at[n, h, pl.ds(0, 3)], send.at[n, h, 2])
            sent(g.at[n, h, pl.ds(0, 15)], send.at[n, h, 3])
            cols = columns(n, h)
            pltpu.make_async_copy(gwb.at[n, h], own_hbm.at[:, cols], out_sem.at[n, h]).wait()
            done = remote(gwb.at[n, h], other_hbm.at[:, cols], dep_send.at[n, h], dep_recv.at[n, h], other)
            done.wait_send()
            done.wait_recv()
    for k in range(8):
        ref = two(0) if k < 6 else tok.at[0, 0]
        sent(ref, z_send.at[k])
    sent(zsend.at[pl.ds(0, 14)], zs_send.at[0])
    act_out.wait()
    gt_out.wait()


def local(tokens, weight, cotangent):
    d, f = weight.shape
    fh = f // (2 * NCH)
    any_spec = pl.BlockSpec(memory_space=pl.ANY)
    vmem = pltpu.VMEM
    dma = pltpu.SemaphoreType.DMA
    act, own, other, gt = pl.pallas_call(
        kernel,
        out_shape=(
            jax.ShapeDtypeStruct(cotangent.shape, BF16),
            jax.ShapeDtypeStruct(weight.shape, BF16),
            jax.ShapeDtypeStruct(weight.shape, BF16),
            jax.ShapeDtypeStruct((2, 64, d), BF16),
        ),
        in_specs=[any_spec] * 3,
        out_specs=(any_spec,) * 4,
        scratch_shapes=[
            vmem(weight.shape, BF16),
            vmem(cotangent.shape, BF16),
            vmem(cotangent.shape, BF16),
            vmem((2, 16, 64, d), BF16),
            vmem((2, SIDE, d, 256), BF16),
            vmem((NCH, 2, 16, 64, fh), BF16),
            vmem((NCH, 2, SIDE, 2, 32, fh), BF16),
            vmem((NCH, 2, SIDE, 2, 64, fh), BF16),
            vmem((NCH, 2, SIDE, 64, fh), BF16),
            vmem((NCH, 2, 2, 32, fh), BF16),
            vmem((NCH, 2, 2, 64, fh), BF16),
            vmem((NCH, 2, 16, 64, fh), BF16),
            vmem((2, d, fh), F32),
            vmem((NCH, 2, d, fh), BF16),
            vmem((16, 64, d), F32),
            vmem((16, 64, d), BF16),
            vmem((ROWS - 1, 2, 64, d), BF16),
            dma((3,)),
            dma((NCH, 2)),
            dma((8,)),
            dma((8,)),
            dma((NCH, 2, 4)),
            dma((NCH, 2, SIDE)),
            dma((NCH, 2, SIDE)),
            dma((NCH, 2)),
            dma((NCH, 2)),
            dma((NCH, 2, SIDE, SIDE)),
            dma((NCH, 2)),
            dma((NCH, 2)),
            dma((1,)),
            dma((1,)),
        ],
        compiler_params=pltpu.CompilerParams(
            collective_id=0, has_side_effects=True, vmem_limit_bytes=56 * 2**20
        ),
    )(tokens.reshape(2, 64, d), weight, cotangent)
    grad_weight = (own.astype(F32) + other.astype(F32)).astype(BF16)
    return (act, gt.reshape(128, d), grad_weight)


def solution(mesh):
    placed = (P(("depth", "row"), "col"), P("col", "row"), P(("depth", "col"), "row"))
    return jax.shard_map(
        local,
        mesh=mesh,
        in_specs=placed,
        out_specs=(P(("depth", "col"), "row"), P(("depth", "row"), "col"), P("col", "row")),
        check_vma=False,
    )
```

time: 287 us -> 125 us (0.44)
  waiting for transfers between devices: 216 us -> 0 us
  Pallas kernels: 0 us -> 116 us
  blocking collectives: 30.2 us -> 0 us
  matrix products: 19.7 us -> 0 us
  between operations: 13.8 us -> 0.66 us
  local copies, waits for them, and re-layouts: 4.28 us -> 1.39 us
    reduce_scatter x2 -> x0, waiting for transfers between devices: 124 us -> none  [the longest x1 85.5 us: local(): lax.psum_scatter(jnp.dot(rows, weight, preferred_element_type=jnp.float32...]
    pallas_call x0 -> x1, Pallas kernels: none -> 116 us  [local(): pl.pallas_call(kernel, out_shape=(jax.ShapeDtypeStruct(cotangent.shape, B...]
    all_gather x1 -> x0, waiting for transfers between devices: 66.8 us -> none  [local(): grad_panel = lax.all_gather(grad_hidden, 'col', axis=0, tiled=True)]
    all_gather x1 -> x0, blocking collectives: 30.2 us -> none  [local(): panel = lax.all_gather(tokens, 'row', axis=0, tiled=True)]
    psum x1 -> x0, waiting for transfers between devices: 25.7 us -> none  [local(): grad_weight = lax.psum(partial_weight.astype(jnp.bfloat16), 'depth')]
    dot_general x3 -> x0, matrix products: 19.7 us -> none  [the longest x1 7.66 us: local(): lax.dot_general(panel, grad_panel, (((0,), (0,)), ((), ())), preferred_el...]
    unnamed x5 -> x6, local copies, waits for them, and re-layouts: 4.28 us -> 1.39 us
  transfers between devices with their start and end apart: 4 -> 0, of which waited for: 4 -> 0; matrix products, arithmetic and copies ran while one was open for 4% -> 0% of each run, Pallas kernels for 0% -> 0%
where the time goes in v1:
time: 125 us; the launch traced here: 123 us
  Pallas kernels  116 us (93%)
  other arithmetic  4.73 us (4%)
  local copies, waits for them, and re-layouts  1.39 us (1%)
    pallas_call x1, Pallas kernels, local(): pl.pallas_call(kernel, out_shape=(jax.ShapeDtypeStruct(cotangent.shape, B...  116 us
    convert_element_type x1, other arithmetic, local(): grad_weight = (own.astype(F32) + other.astype(F32)).astype(BF16)  4.73 us

profile of v1, /device:TPU:4, one launch (start us, length us, event | category | flops | bytes accessed | tf_op | source)
XLA Modules:
  0.0 123.1 jit_solution(11108407537377489965)
XLA Ops:
  0.6 116.3 %shard_map.58 = (bf16[64,3072]{1,0:T(8,128)(2,1)}, bf16[384,3072]{1,0:T(8,128)(2,1)}, bf16[384,3072]{1,0:T(8,128)(2,1)}, bf16[2,64,384]{2,1,0:T(8,128)(2,1)}) custom-call(bf16[2,64,384]{2,1,0:T(8,128)(2,1)} %bitcast.2, bf16[384,3072]{1,0:T(8,128)(2,1)} %w_hbm.1, bf16[64,3072]{1,0:T(8,128)(2,1)} %cot_hbm.1), custom_call_target="tpu_custom_call" | custom-call | tf_op jit(solution)/shard_map/pallas_call | solution.py:358
  116.9 0.0 copy-start
  116.9 0.0 copy-start.1
  117.0 4.7 %add_convert_fusion = bf16[384,3072]{1,0:T(8,128)(2,1)} fusion(bf16[384,3072]{1,0:T(8,128)(2,1)} %get-tuple-element.10, bf16[384,3072]{1,0:T(8,128)(2,1)} %get-tuple-element.9), kind=kLoop, calls=%fused_computation | loop fusion | flops 4718592 | bytes 7077888 | tf_op jit(solution)/shard_map/convert_element_type | solution.py:405
  121.7 0.0 copy-done
  121.7 0.7 copy.8
  122.4 0.0 copy-done.1
  122.4 0.6 copy.9
Async XLA Ops:
  116.9 4.7 %copy-start = (bf16[64,3072]{1,0:T(8,128)(2,1)S(1)}, bf16[64,3072]{1,0:T(8,128)(2,1)}, u32[]{:S(2)}) copy-start(bf16[64,3072]{1,0:T(8,128)(2,1)} %get-tuple-element.14) | copy-start | bytes 1179652
  116.9 5.5 %copy-start.1 = (bf16[2,64,384]{2,1,0:T(8,128)(2,1)S(1)}, bf16[2,64,384]{2,1,0:T(8,128)(2,1)}, u32[]{:S(2)}) copy-start(bf16[2,64,384]{2,1,0:T(8,128)(2,1)} %get-tuple-element.8) | copy-start | bytes 294916

commit v2 on v1

v2 whole, which is shorter than its diff:
```python
import functools
import math

import jax
import jax.numpy as jnp
from jax import lax
from jax.experimental import pallas as pl
from jax.experimental.pallas import tpu as pltpu
from jax.sharding import PartitionSpec as P

MESH = pl.DeviceIdType.MESH
NCH = 2
SIDE = 4
ROWS = 8
BF16 = jnp.bfloat16
F32 = jnp.float32


def gelu_parts(hidden):
    cdf = 0.5 * (1.0 + lax.erf(hidden * (1.0 / math.sqrt(2.0))))
    density = jnp.exp(-0.5 * hidden * hidden) * (1.0 / math.sqrt(2.0 * math.pi))
    return (cdf, density)


GATHERS = ((0, 0, 64, False), (1, 0, 32, False), (1, 32, 32, False))


def schedule():
    t = [("Z", 0, 1), ("IW", 0, 0), ("Z", 0, 2), ("IW", 0, 1), ("FP", 0, 0), ("FQ", 0, 0)]
    t += [("Z", 0, 3), ("IW", 0, 2), ("FP", 0, 1), ("FQ", 0, 1), ("DP", 0, 0)]
    t += [("Z", 0, 4), ("IW", 0, 3), ("FP", 0, 2), ("FQ", 0, 2), ("DP", 0, 1), ("tokens", 0, 0)]
    t += [("I", 1, 2), ("FP", 0, 3), ("FQ", 0, 3), ("I", 1, 1), ("DP", 0, 2), ("DQ", 0, 2)]
    t += [("I", 1, 3), ("DQ", 0, 1), ("DP", 0, 3), ("I", 1, 0), ("DQ", 0, 3), ("DQ", 0, 0)]
    t += [("F2", 0, 0), ("D2", 0, 0), ("S", 0, 0), ("transposes", 0, 0)]
    t += [("F", 1, 2), ("F", 1, 1), ("A1", 0, 0), ("D", 1, 2), ("F", 1, 3), ("D", 1, 1)]
    t += [("B", 0, 0), ("F", 1, 0), ("A2", 0, 0), ("D", 1, 3), ("D", 1, 0)]
    t += [("B", 0, 1), ("B", 0, 3), ("F2", 1, 0), ("T", 0, 0), ("B", 0, 2)]
    t += [("D2", 1, 0), ("S", 1, 0), ("S", 2, 0)]
    t += [("T", 0, 1), ("A1", 1, 0), ("T", 0, 3), ("A1", 2, 0), ("B", 1, 0), ("T", 0, 2), ("W", 0, 0)]
    t += [("A2", 1, 0), ("B", 2, 0), ("A2", 2, 0), ("B", 1, 1), ("B", 1, 3), ("B", 2, 1), ("B", 2, 3)]
    t += [("T", 1, 0), ("B", 1, 2), ("T", 2, 0), ("B", 2, 2), ("T", 1, 1), ("T", 1, 3), ("T", 1, 2)]
    t += [("W", 1, 0), ("T", 2, 1), ("T", 2, 3), ("T", 2, 2), ("W", 2, 0)]
    return t


def kernel(
    tok_hbm, w_hbm, cot_hbm, act_hbm, own_hbm, other_hbm, gt_hbm,
    w, cot, act, tok, tok_t, part, f1, r1, s, f2, r2, g, gw, gwb, gt, zsend, zrecv,
    local_sem, out_sem, z_send, z_recv, send, g_send, f1_sem, r1_sem, f2_sem, r2_sem, g_sem,
    dep_send, dep_recv, zs_send, zs_recv,
):
    fh = part.shape[-1]
    half = 32
    depth, row, col = (lax.axis_index(a) for a in ("depth", "row", "col"))
    yx = (col // SIDE, col % SIDE)
    lo, hi = pl.ds(0, half), pl.ds(half, half)

    loads = [
        pltpu.make_async_copy(tok_hbm, tok.at[0, pl.ds(2 * row, 2)], local_sem.at[0]),
        pltpu.make_async_copy(w_hbm, w, local_sem.at[1]),
        pltpu.make_async_copy(cot_hbm, cot, local_sem.at[2]),
    ]
    for load in loads:
        load.start()

    def grid_device(axis, delta):
        at = list(yx)
        at[axis] = (at[axis] + delta + SIDE) % SIDE
        return {"col": at[0] * SIDE + at[1]}

    def row_device(delta):
        return {"row": (row + delta + ROWS) % ROWS}

    other = {"depth": 1 - depth}

    barrier = pltpu.get_barrier_semaphore()
    peers = [row_device(d) for d in range(1, ROWS)]
    peers += [grid_device(axis, delta) for axis in (0, 1) for delta in (1, 2, 3)]
    peers += [other]
    for peer in peers:
        pl.semaphore_signal(barrier, inc=1, device_id=peer, device_id_type=MESH)
    loads[0].wait()
    pl.semaphore_wait(barrier, len(peers))

    def remote(src, dst, ssem, rsem, device):
        return pltpu.make_async_remote_copy(
            src_ref=src, dst_ref=dst, send_sem=ssem, recv_sem=rsem,
            device_id=device, device_id_type=MESH,
        )

    def push(src, dst, ssem, rsem, device):
        remote(src, dst, ssem, rsem, device).start()

    def arrived(ref, rsem):
        remote(ref, ref, send.at[0, 0, 0], rsem, other).wait_recv()

    def sent(ref, ssem):
        remote(ref, ref, ssem, f2_sem.at[0, 0], other).wait_send()

    def piece(delta, k):
        return tok.at[0, 2 * ((row + delta + ROWS) % ROWS) + k]

    def hand_on(delta, k, way):
        sem = 4 * abs(delta) + 2 * k + way
        push(piece(delta, k), piece(delta, k), z_send.at[sem], z_recv.at[sem], row_device(1 - 2 * way))

    for k in (0, 1):
        hand_on(0, k, 0)
        hand_on(0, k, 1)
    gt[...] = jnp.zeros_like(gt)

    def task_z(step):
        for k in (0, 1):
            for way in (0, 1):
                if step == 4 and k != way:
                    continue
                delta = -step if way == 0 else step
                arrived(piece(delta, k), z_recv.at[4 * (step - 1) + 2 * k + way])
                if step < 3 or (step == 3 and k == way):
                    hand_on(delta, k, way)

    def task_tokens():
        for at_y in range(SIDE):
            for at_x in range(SIDE):
                tok[1, at_x * SIDE + at_y] = tok[0, at_y * SIDE + at_x]

    def task_transposes():
        for h in range(2):
            for t in range(2):
                tok_t[h, t] = tok[h, :, pl.ds(32 * t, 32)].reshape(512, 384).T

    def ring(h):
        axis_a, axis_b = (1, 0) if h == 0 else (0, 1)
        return axis_a, axis_b, yx[axis_a], yx[axis_b]

    def slot(h, j, i):
        _, _, a, b = ring(h)
        return ((b + j) % SIDE) * SIDE + (a + i) % SIDE

    def columns(n, h):
        return pl.ds((2 * n + h) * fh, fh)

    def group(h, j):
        _, _, _, b = ring(h)
        return (b + j) % SIDE

    toward = 1 - 2 * (row % 2)
    waves = [row // 2, (row // 2 - toward + SIDE) % SIDE, (row // 2 + toward + SIDE) % SIDE, (row // 2 + 2) % SIDE]

    def first_sends(n, h, j):
        axis_a = ring(h)[0]
        right, left = grid_device(axis_a, 1), grid_device(axis_a, -1)
        ssem = send.at[n, h, 0]
        far = part.at[n, h, slot(h, j, 2)]
        push(far.at[lo], f1.at[n, h, j, 0], ssem, f1_sem.at[n, h, j, 0], right)
        push(far.at[hi], f1.at[n, h, j, 1], ssem, f1_sem.at[n, h, j, 1], left)
        push(part.at[n, h, slot(h, j, 1), hi], r1.at[n, h, j, 0, hi], ssem, r1_sem.at[n, h, j], right)
        push(part.at[n, h, slot(h, j, 3), lo], r1.at[n, h, j, 1, lo], ssem, r1_sem.at[n, h, j], left)

    def task_iw(n, wave):
        at_y = waves[wave]
        if wave == 0:
            loads[1].wait()
        four = pl.ds(SIDE * at_y, SIDE)
        x = tok[0, four].reshape(256, 384)
        y = jnp.dot(x, w[:, columns(n, 0)], preferred_element_type=F32).astype(BF16)
        part[n, 0, four] = y.reshape(SIDE, 64, fh)
        first_sends(n, 0, (at_y - yx[0] + SIDE) % SIDE)
        y = jnp.dot(x, w[:, columns(n, 1)], preferred_element_type=F32).astype(BF16)
        for at_x in range(SIDE):
            part[n, 1, SIDE * at_x + at_y] = y[64 * at_x : 64 * at_x + 64]
        role = (at_y - yx[0] + SIDE) % SIDE
        right, left = grid_device(0, 1), grid_device(0, -1)
        ssem = send.at[n, 1, 0]

        @pl.when(role == 2)
        def _():
            for j in range(SIDE):
                far = part.at[n, 1, slot(1, j, 2)]
                push(far.at[lo], f1.at[n, 1, j, 0], ssem, f1_sem.at[n, 1, j, 0], right)
                push(far.at[hi], f1.at[n, 1, j, 1], ssem, f1_sem.at[n, 1, j, 1], left)

        @pl.when(role == 1)
        def _():
            for j in range(SIDE):
                push(part.at[n, 1, slot(1, j, 1), hi], r1.at[n, 1, j, 0, hi], ssem, r1_sem.at[n, 1, j], right)

        @pl.when(role == 3)
        def _():
            for j in range(SIDE):
                push(part.at[n, 1, slot(1, j, 3), lo], r1.at[n, 1, j, 1, lo], ssem, r1_sem.at[n, 1, j], left)

    def task_i(n, h, j):
        four = pl.ds(SIDE * group(h, j), SIDE)
        x = tok[h, four].reshape(256, 384)
        y = jnp.dot(x, w[:, columns(n, h)], preferred_element_type=F32).astype(BF16)
        part[n, h, four] = y.reshape(SIDE, 64, fh)
        first_sends(n, h, j)

    def forward(n, h, j, way):
        axis_a = ring(h)[0]
        device = grid_device(axis_a, 1 - 2 * way)
        rows, near = (lo, 1) if way == 0 else (hi, 3)
        arrived(f1.at[n, h, j, way], f1_sem.at[n, h, j, way])
        f1[n, h, j, way] = (
            f1[n, h, j, way].astype(F32) + part[n, h, slot(h, j, near), rows].astype(F32)
        ).astype(BF16)
        push(f1.at[n, h, j, way], r1.at[n, h, j, way, rows], send.at[n, h, 1], r1_sem.at[n, h, j], device)

    def task_f(n, h, j):
        forward(n, h, j, 0)
        forward(n, h, j, 1)

    def task_fq(n, wave):
        role = (waves[wave] - yx[0] + SIDE) % SIDE

        @pl.when(role == 1)
        def _():
            for j in range(SIDE):
                forward(n, 1, j, 0)

        @pl.when(role == 3)
        def _():
            for j in range(SIDE):
                forward(n, 1, j, 1)

    def sum_first(n, h, j):
        arrived(r1.at[n, h, j], r1_sem.at[n, h, j])
        total = part[n, h, slot(h, j, 0)].astype(F32)
        total = total + r1[n, h, j, 0].astype(F32) + r1[n, h, j, 1].astype(F32)
        s[n, h, j] = total.astype(BF16)

    def second_sends(n, h, j):
        axis_b = ring(h)[1]
        right, left = grid_device(axis_b, 1), grid_device(axis_b, -1)
        ssem = send.at[n, h, 2]
        if j == 2:
            push(s.at[n, h, 2, lo], f2.at[n, h, 0], ssem, f2_sem.at[n, h], right)
            push(s.at[n, h, 2, hi], f2.at[n, h, 1], ssem, f2_sem.at[n, h], left)
        elif j == 1:
            push(s.at[n, h, 1, hi], r2.at[n, h, 0, hi], ssem, r2_sem.at[n, h], right)
        elif j == 3:
            push(s.at[n, h, 3, lo], r2.at[n, h, 1, lo], ssem, r2_sem.at[n, h], left)

    def task_d(n, h, j):
        sum_first(n, h, j)
        second_sends(n, h, j)

    def task_dp(n, wave):
        j = (waves[wave] - yx[0] + SIDE) % SIDE
        sum_first(n, 0, j)
        for role in (1, 2, 3):
            pl.when(j == role)(functools.partial(second_sends, n, 0, role))

    def task_f2(n, h):
        axis_b = ring(h)[1]
        right, left = grid_device(axis_b, 1), grid_device(axis_b, -1)
        ssem = send.at[n, h, 2]
        arrived(f2.at[n, h], f2_sem.at[n, h])
        f2[n, h, 0] = (f2[n, h, 0].astype(F32) + s[n, h, 1, lo].astype(F32)).astype(BF16)
        push(f2.at[n, h, 0], r2.at[n, h, 0, lo], ssem, r2_sem.at[n, h], right)
        f2[n, h, 1] = (f2[n, h, 1].astype(F32) + s[n, h, 3, hi].astype(F32)).astype(BF16)
        push(f2.at[n, h, 1], r2.at[n, h, 1, hi], ssem, r2_sem.at[n, h], left)

    def task_d2(n, h):
        arrived(r2.at[n, h], r2_sem.at[n, h])
        mine = slot(h, 0, 0)

        @pl.loop(0, 4)
        def _(at):
            rows = pl.ds(pl.multiple_of(at * 16, 16), 16)
            hidden = s[n, h, 0, rows].astype(F32) + r2[n, h, 0, rows].astype(F32) + r2[n, h, 1, rows].astype(F32)
            cdf, density = gelu_parts(hidden)
            act[rows, columns(n, h)] = (hidden * cdf).astype(BF16)
            grad = cot[rows, columns(n, h)].astype(F32) * (cdf + hidden * density)
            g[n, h, mine, rows] = grad.astype(BF16)

    def block(c, h, j, i):
        n, start, size, _ = GATHERS[c]
        return g.at[n, h, slot(h, j, i), pl.ds(start, size)]

    def share(c, h, j, i, axis, delta):
        n, start, size, straight = GATHERS[c]
        axis_a = ring(h)[0]
        nj, ni = (j, (i - delta) % SIDE) if axis == axis_a else ((j - delta) % SIDE, i)
        ref = block(c, h, j, i)
        if delta != 2 and 2 in (ni if axis == axis_a else nj,):
            ref = g.at[n, h, slot(h, j, i), pl.ds(start if delta == 1 else start + size // 2, size // 2)]
        push(ref, ref, g_send.at[c, h], g_sem.at[c, h, nj, ni], grid_device(axis, delta))

    def ways(c):
        return (1, -1, 2) if GATHERS[c][3] else (1, -1)

    here = set()

    def block_here(c, h, j, i):
        if (c, h, j, i) not in here:
            here.add((c, h, j, i))
            arrived(block(c, h, j, i), g_sem.at[c, h, j, i])

    def task_s(c, h):
        axis_a, axis_b, _, _ = ring(h)
        here.add((c, h, 0, 0))
        for axis in (axis_b, axis_a):
            for delta in ways(c):
                share(c, h, 0, 0, axis, delta)

    def task_a1(c, h):
        axis_a, axis_b, _, _ = ring(h)
        for j, delta in ((3, 1), (1, -1)):
            block_here(c, h, j, 0)
            if not GATHERS[c][3]:
                share(c, h, j, 0, axis_b, delta)
        for j in (3, 1):
            for delta in ways(c):
                share(c, h, j, 0, axis_a, delta)

    def task_a2(c, h):
        axis_a = ring(h)[0]
        block_here(c, h, 2, 0)
        for delta in ways(c):
            share(c, h, 2, 0, axis_a, delta)

    def task_b(c, h, j):
        axis_a = ring(h)[0]
        if not GATHERS[c][3]:
            block_here(c, h, j, 3)
            share(c, h, j, 3, axis_a, 1)
            block_here(c, h, j, 1)
            share(c, h, j, 1, axis_a, -1)

    finished = set()

    def task_t(c, h, i):
        n, start, size, _ = GATHERS[c]
        rows = pl.ds(start, size)
        at_x = (yx[1] + i) % SIDE
        for k in range(SIDE):
            block_here(c, h, *((k, i) if h == 0 else (i, k)))
        if h == 0:
            blocks = jnp.concatenate([g[n, h, SIDE * at_y + at_x, rows] for at_y in range(SIDE)], axis=0)
        else:
            blocks = g[n, h, pl.ds(SIDE * at_x, SIDE), rows].reshape(SIDE * size, fh)
        terms = lax.dot_general(
            blocks, w[:, columns(n, h)], (((1,), (1,)), ((), ())), preferred_element_type=F32
        )
        for at_y in range(SIDE):
            at = SIDE * at_y + at_x
            gt[at, rows] = gt[at, rows] + terms[size * at_y : size * at_y + size]
        finished.add((c, h, i))
        if n == NCH - 1 and (c, 1 - h, i) in finished:
            for at_y in range(SIDE):
                send_tokens(SIDE * at_y + at_x, rows)

    def send_tokens(at, rows):
        zsend[at, rows] = gt[at, rows].astype(BF16)
        to = at // 2
        ahead = (to - row + ROWS) % ROWS

        @pl.when(ahead != 0)
        def _():
            place = ROWS - 1 - ahead
            push(zsend.at[at, rows], zrecv.at[place, at % 2, rows], zs_send.at[0], zs_recv.at[0], {"row": to})

    def task_w(c, h):
        n, start, size, _ = GATHERS[c]
        for j in range(SIDE):
            for i in range(SIDE):
                block_here(c, h, j, i)
        total = None
        for t in range(start // half, (start + size) // half):
            rows = g[n, h, :, pl.ds(half * t, half)].reshape(512, fh)
            term = jnp.dot(tok_t[h, t], rows, preferred_element_type=F32)
            total = term if total is None else total + term
        if start > 0:
            total = gw[h] + total
        if start + size < 64:
            gw[h] = total
        else:
            gwb[n, h] = total.astype(BF16)
            cols = columns(n, h)
            push(gwb.at[n, h], other_hbm.at[:, cols], dep_send.at[n, h], dep_recv.at[n, h], other)
            pltpu.make_async_copy(gwb.at[n, h], own_hbm.at[:, cols], out_sem.at[n, h]).start()

    both = {"F": task_f, "D": task_d, "I": task_i, "B": task_b, "T": task_t}
    both_once = {"F2": task_f2, "D2": task_d2, "S": task_s, "A1": task_a1, "A2": task_a2, "W": task_w}
    cot_waited = False
    for name, n, j in schedule():
        if name == "D2" and not cot_waited:
            loads[2].wait()
            cot_waited = True
        if name in both:
            for h in (0, 1):
                both[name](n, h, j)
        elif name in both_once:
            for h in (0, 1):
                both_once[name](n, h)
        elif name == "Z":
            task_z(j)
        elif name == "IW":
            task_iw(n, j)
        elif name == "FP":
            task_f(n, 0, (waves[j] - yx[0] + SIDE) % SIDE)
        elif name == "FQ":
            task_fq(n, j)
        elif name == "DP":
            task_dp(n, j)
        elif name == "DQ":
            task_d(n, 1, j)
        elif name == "tokens":
            task_tokens()
        elif name == "transposes":
            task_transposes()

    act_out = pltpu.make_async_copy(act, act_hbm, local_sem.at[0])
    act_out.start()
    arrived(zrecv, zs_recv.at[0])
    for at in range(2):
        total = gt[2 * row + at].astype(BF16).astype(F32)
        for place in range(ROWS - 1):
            total = total + zrecv[place, at].astype(F32)
        zsend[2 * row + at] = total.astype(BF16)
    gt_out = pltpu.make_async_copy(zsend.at[pl.ds(2 * row, 2)], gt_hbm, local_sem.at[1])
    gt_out.start()

    for n in range(NCH):
        for h in (0, 1):
            sent(r1.at[n, h], send.at[n, h, 0])
            sent(s.at[n, h], send.at[n, h, 1])
            sent(s.at[n, h, pl.ds(0, 3)], send.at[n, h, 2])
            cols = columns(n, h)
            pltpu.make_async_copy(gwb.at[n, h], own_hbm.at[:, cols], out_sem.at[n, h]).wait()
            done = remote(gwb.at[n, h], other_hbm.at[:, cols], dep_send.at[n, h], dep_recv.at[n, h], other)
            done.wait_send()
            done.wait_recv()
    for c, (n, start, size, _) in enumerate(GATHERS):
        for h in (0, 1):
            sent(g.at[n, h, pl.ds(0, 15), pl.ds(start, size)], g_send.at[c, h])
    for delta in range(4):
        for k in (0, 1):
            for way in (0, 1):
                if delta < 3 or k == way:
                    sent(tok.at[0, 0], z_send.at[4 * delta + 2 * k + way])
    sent(zsend.at[pl.ds(0, 14)], zs_send.at[0])
    act_out.wait()
    gt_out.wait()


def local(tokens, weight, cotangent):
    d, f = weight.shape
    fh = f // (2 * NCH)
    any_spec = pl.BlockSpec(memory_space=pl.ANY)
    vmem = pltpu.VMEM
    dma = pltpu.SemaphoreType.DMA
    act, own, other, gt = pl.pallas_call(
        kernel,
        out_shape=(
            jax.ShapeDtypeStruct(cotangent.shape, BF16),
            jax.ShapeDtypeStruct(weight.shape, BF16),
            jax.ShapeDtypeStruct(weight.shape, BF16),
            jax.ShapeDtypeStruct((2, 64, d), BF16),
        ),
        in_specs=[any_spec] * 3,
        out_specs=(any_spec,) * 4,
        scratch_shapes=[
            vmem(weight.shape, BF16),
            vmem(cotangent.shape, BF16),
            vmem(cotangent.shape, BF16),
            vmem((2, 16, 64, d), BF16),
            vmem((2, 2, d, 512), BF16),
            vmem((NCH, 2, 16, 64, fh), BF16),
            vmem((NCH, 2, SIDE, 2, 32, fh), BF16),
            vmem((NCH, 2, SIDE, 2, 64, fh), BF16),
            vmem((NCH, 2, SIDE, 64, fh), BF16),
            vmem((NCH, 2, 2, 32, fh), BF16),
            vmem((NCH, 2, 2, 64, fh), BF16),
            vmem((NCH, 2, 16, 64, fh), BF16),
            vmem((2, d, fh), F32),
            vmem((NCH, 2, d, fh), BF16),
            vmem((16, 64, d), F32),
            vmem((16, 64, d), BF16),
            vmem((ROWS - 1, 2, 64, d), BF16),
            dma((3,)),
            dma((NCH, 2)),
            dma((16,)),
            dma((16,)),
            dma((NCH, 2, 3)),
            dma((len(GATHERS), 2)),
            dma((NCH, 2, SIDE, 2)),
            dma((NCH, 2, SIDE)),
            dma((NCH, 2)),
            dma((NCH, 2)),
            dma((len(GATHERS), 2, SIDE, SIDE)),
            dma((NCH, 2)),
            dma((NCH, 2)),
            dma((1,)),
            dma((1,)),
        ],
        compiler_params=pltpu.CompilerParams(
            collective_id=0, has_side_effects=True, vmem_limit_bytes=48 * 2**20
        ),
    )(tokens.reshape(2, 64, d), weight, cotangent)
    grad_weight = (own.astype(F32) + other.astype(F32)).astype(BF16)
    return (act, gt.reshape(128, d), grad_weight)


def solution(mesh):
    placed = (P(("depth", "row"), "col"), P("col", "row"), P(("depth", "col"), "row"))
    return jax.shard_map(
        local,
        mesh=mesh,
        in_specs=placed,
        out_specs=(P(("depth", "col"), "row"), P(("depth", "row"), "col"), P("col", "row")),
        check_vma=False,
    )
```

time: 125 us -> 108 us (0.86); the launches traced: 123 us -> 108 us
  Pallas kernels: 116 us -> 102 us
  other arithmetic: 4.73 us -> 2.29 us
  local copies, waits for them, and re-layouts: 1.39 us -> 3.27 us
    pallas_call x1, Pallas kernels: 116 us -> 102 us  [local(): pl.pallas_call(kernel, out_shape=(jax.ShapeDtypeStruct(cotangent.shape, B...]
    convert_element_type x1, other arithmetic: 4.73 us -> 2.29 us  [local(): grad_weight = (own.astype(F32) + other.astype(F32)).astype(BF16)]
    unnamed x6, local copies, waits for them, and re-layouts: 1.39 us -> 3.27 us
where the time goes in v2:
time: 108 us
  Pallas kernels  102 us (94%)
  local copies, waits for them, and re-layouts  3.27 us (3%)
  other arithmetic  2.29 us (2%)
    pallas_call x1, Pallas kernels, local(): pl.pallas_call(kernel, out_shape=(jax.ShapeDtypeStruct(cotangent.shape, B...  102 us
    unnamed x6, local copies, waits for them, and re-layouts  3.27 us
    convert_element_type x1, other arithmetic, local(): grad_weight = (own.astype(F32) + other.astype(F32)).astype(BF16)  2.29 us

profile of v2, /device:TPU:4, one launch (start us, length us, event | category | flops | bytes accessed | tf_op | source)
XLA Modules:
  0.0 107.8 jit_solution(10745195552170098154)
XLA Ops:
  0.6 0.0 copy-start
  0.6 1.0 copy-done
  1.6 0.0 copy-start.1
  1.6 0.9 copy-done.1
  2.5 101.6 %shard_map.58 = (bf16[64,3072]{1,0:T(8,128)(2,1)S(1)}, bf16[384,3072]{1,0:T(8,128)(2,1)S(1)}, bf16[384,3072]{1,0:T(8,128)(2,1)S(1)}, bf16[2,64,384]{2,1,0:T(8,128)(2,1)S(1)}) custom-call(bf16[2,64,384]{2,1,0:T(8,128)(2,1)S(1)} %bitcast.2, bf16[384,3072]{1,0:T(8,128)(2,1)} %w_hbm.1, bf16[64,3072]{1,0:T(8,128)(2,1)S(1)} %copy-done), custom_call_target="tpu_custom_call" | custom-call | tf_op jit(solution)/shard_map/pallas_call | solution.py:455
  104.1 2.3 %add_convert_fusion = bf16[384,3072]{1,0:T(8,128)(2,1)} fusion(bf16[384,3072]{1,0:T(8,128)(2,1)S(1)} %get-tuple-element.10, bf16[384,3072]{1,0:T(8,128)(2,1)S(1)} %get-tuple-element.9), kind=kLoop, calls=%fused_computation | loop fusion | flops 4718592 | bytes 7077888 | tf_op jit(solution)/shard_map/convert_element_type | solution.py:503
  106.4 0.7 copy.8
  107.1 0.6 copy.9
Async XLA Ops:
  0.6 1.0 copy-start
  1.6 0.9 copy-start.1

commit v3 on v2

--- a/solution.py
+++ b/solution.py
@@ -10,6 +10,7 @@
 
 MESH = pl.DeviceIdType.MESH
 NCH = 2
+X_FIRST = (3, 2)
 SIDE = 4
 ROWS = 8
 BF16 = jnp.bfloat16
@@ -22,25 +23,27 @@
     return (cdf, density)
 
 
-GATHERS = ((0, 0, 64, False), (1, 0, 32, False), (1, 32, 32, False))
-
-
-def schedule():
-    t = [("Z", 0, 1), ("IW", 0, 0), ("Z", 0, 2), ("IW", 0, 1), ("FP", 0, 0), ("FQ", 0, 0)]
-    t += [("Z", 0, 3), ("IW", 0, 2), ("FP", 0, 1), ("FQ", 0, 1), ("DP", 0, 0)]
-    t += [("Z", 0, 4), ("IW", 0, 3), ("FP", 0, 2), ("FQ", 0, 2), ("DP", 0, 1), ("tokens", 0, 0)]
-    t += [("I", 1, 2), ("FP", 0, 3), ("FQ", 0, 3), ("I", 1, 1), ("DP", 0, 2), ("DQ", 0, 2)]
-    t += [("I", 1, 3), ("DQ", 0, 1), ("DP", 0, 3), ("I", 1, 0), ("DQ", 0, 3), ("DQ", 0, 0)]
-    t += [("F2", 0, 0), ("D2", 0, 0), ("S", 0, 0), ("transposes", 0, 0)]
-    t += [("F", 1, 2), ("F", 1, 1), ("A1", 0, 0), ("D", 1, 2), ("F", 1, 3), ("D", 1, 1)]
-    t += [("B", 0, 0), ("F", 1, 0), ("A2", 0, 0), ("D", 1, 3), ("D", 1, 0)]
-    t += [("B", 0, 1), ("B", 0, 3), ("F2", 1, 0), ("T", 0, 0), ("B", 0, 2)]
-    t += [("D2", 1, 0), ("S", 1, 0), ("S", 2, 0)]
-    t += [("T", 0, 1), ("A1", 1, 0), ("T", 0, 3), ("A1", 2, 0), ("B", 1, 0), ("T", 0, 2), ("W", 0, 0)]
-    t += [("A2", 1, 0), ("B", 2, 0), ("A2", 2, 0), ("B", 1, 1), ("B", 1, 3), ("B", 2, 1), ("B", 2, 3)]
-    t += [("T", 1, 0), ("B", 1, 2), ("T", 2, 0), ("B", 2, 2), ("T", 1, 1), ("T", 1, 3), ("T", 1, 2)]
-    t += [("W", 1, 0), ("T", 2, 1), ("T", 2, 3), ("T", 2, 2), ("W", 2, 0)]
-    return t
+GATHERS = ((0, 0, 64, False), (1, 0, 64, False))
+
+
+ORDER = (
+    ("Z", 0, 1), ("IW", 0, 0), ("FP", 0, 0), ("Z", 0, 2), ("IW", 0, 1), ("DP", 0, 0), ("FP", 0, 1),
+    ("Z", 0, 3), ("Z", 0, 4), ("IW", 0, 2), ("IW", 0, 3), ("tokens", 0, 0), ("I1", 0, 0), ("I1", 0, 1),
+    ("I1", 0, 2), ("I1", 0, 3), ("DP", 0, 1), ("I0", 1, 0), ("I0", 1, 1), ("I0", 1, 2), ("I0", 1, 3),
+    ("FP", 0, 2), ("F1", 0, 0), ("I1", 1, 0), ("I1", 1, 1), ("F1", 0, 1), ("I1", 1, 2), ("I1", 1, 3),
+    ("F1", 0, 2), ("transposes", 0, 0), ("FP", 0, 3), ("F1", 0, 3), ("D1", 0, 0), ("F0", 1, 0), ("F1", 1, 0),
+    ("F0", 1, 1), ("F1", 1, 1), ("F0", 1, 2), ("D1", 0, 1), ("F1", 1, 2), ("F0", 1, 3), ("F1", 1, 3),
+    ("DP", 0, 2), ("D1", 0, 2), ("D1", 0, 3), ("DP", 0, 3), ("D1", 1, 0), ("D0", 1, 0), ("D1", 1, 1),
+    ("D0", 1, 1), ("D1", 1, 2), ("D0", 1, 2), ("D1", 1, 3), ("D0", 1, 3), ("G0", 0, 0), ("G1", 0, 0),
+    ("G0", 1, 0), ("G1", 1, 0), ("H1", 0, 0), ("H0", 0, 0), ("S0", 0, 0), ("S1", 0, 0), ("H0", 1, 0),
+    ("H1", 1, 0), ("S0", 1, 0), ("S1", 1, 0), ("A0", 0, 1), ("B0", 0, 0), ("B1", 0, 0), ("A1", 0, 1),
+    ("A0", 1, 1), ("B0", 1, 0), ("B1", 1, 0), ("A1", 1, 1), ("A0", 0, 2), ("T0", 0, 0), ("T1", 0, 0),
+    ("B0", 0, 3), ("B1", 0, 3), ("B0", 0, 1), ("B1", 0, 1), ("A1", 0, 2), ("A0", 1, 2), ("T0", 1, 0),
+    ("T1", 1, 0), ("B0", 1, 3), ("B1", 1, 3), ("B0", 1, 1), ("B1", 1, 1), ("A1", 1, 2), ("T1", 0, 3),
+    ("T1", 0, 1), ("B0", 0, 2), ("T0", 0, 1), ("T0", 0, 3), ("B1", 0, 2), ("T1", 1, 3), ("T1", 1, 1),
+    ("B0", 1, 2), ("T0", 1, 1), ("T0", 1, 3), ("B1", 1, 2), ("T1", 0, 2), ("T0", 0, 2), ("W0", 0, 0),
+    ("T0", 1, 2), ("T1", 1, 2), ("W1", 0, 0), ("W0", 1, 0), ("W1", 1, 0),
+)
 
 
 def kernel(
@@ -49,7 +52,7 @@
     local_sem, out_sem, z_send, z_recv, send, g_send, f1_sem, r1_sem, f2_sem, r2_sem, g_sem,
     dep_send, dep_recv, zs_send, zs_recv,
 ):
-    fh = part.shape[-1]
+    fh = g.shape[-1]
     half = 32
     depth, row, col = (lax.axis_index(a) for a in ("depth", "row", "col"))
     yx = (col // SIDE, col % SIDE)
@@ -100,9 +103,10 @@
     def piece(delta, k):
         return tok.at[0, 2 * ((row + delta + ROWS) % ROWS) + k]
 
-    def hand_on(delta, k, way):
-        sem = 4 * abs(delta) + 2 * k + way
-        push(piece(delta, k), piece(delta, k), z_send.at[sem], z_recv.at[sem], row_device(1 - 2 * way))
+    def hand_on(delta, k, way, far=1):
+        sem = 4 * (abs(delta) + far - 1) + 2 * k + way
+        device = row_device(far * (1 - 2 * way))
+        push(piece(delta, k), piece(delta, k), z_send.at[sem], z_recv.at[sem], device)
 
     for k in (0, 1):
         hand_on(0, k, 0)
@@ -116,8 +120,10 @@
                     continue
                 delta = -step if way == 0 else step
                 arrived(piece(delta, k), z_recv.at[4 * (step - 1) + 2 * k + way])
-                if step < 3 or (step == 3 and k == way):
+                if step < 3:
                     hand_on(delta, k, way)
+                if step == 2 and k == way:
+                    hand_on(delta, k, way, 2)
 
     def task_tokens():
         for at_y in range(SIDE):
@@ -140,6 +146,10 @@
     def columns(n, h):
         return pl.ds((2 * n + h) * fh, fh)
 
+    def summed(n, h):
+        width = part[n][h].shape[-1]
+        return pl.ds(2 * n * fh + (0 if h == 0 else 2 * fh - width), width)
+
     def group(h, j):
         _, _, _, b = ring(h)
         return (b + j) % SIDE
@@ -151,96 +161,55 @@
         axis_a = ring(h)[0]
         right, left = grid_device(axis_a, 1), grid_device(axis_a, -1)
         ssem = send.at[n, h, 0]
-        far = part.at[n, h, slot(h, j, 2)]
-        push(far.at[lo], f1.at[n, h, j, 0], ssem, f1_sem.at[n, h, j, 0], right)
-        push(far.at[hi], f1.at[n, h, j, 1], ssem, f1_sem.at[n, h, j, 1], left)
-        push(part.at[n, h, slot(h, j, 1), hi], r1.at[n, h, j, 0, hi], ssem, r1_sem.at[n, h, j], right)
-        push(part.at[n, h, slot(h, j, 3), lo], r1.at[n, h, j, 1, lo], ssem, r1_sem.at[n, h, j], left)
+        far = part[n][h].at[slot(h, j, 2)]
+        push(far.at[lo], f1[n][h].at[j, 0], ssem, f1_sem.at[n, h, j, 0], right)
+        push(far.at[hi], f1[n][h].at[j, 1], ssem, f1_sem.at[n, h, j, 1], left)
+        push(part[n][h].at[slot(h, j, 1), hi], r1[n][h].at[j, 0, hi], ssem, r1_sem.at[n, h, j], right)
+        push(part[n][h].at[slot(h, j, 3), lo], r1[n][h].at[j, 1, lo], ssem, r1_sem.at[n, h, j], left)
 
     def task_iw(n, wave):
-        at_y = waves[wave]
         if wave == 0:
             loads[1].wait()
-        four = pl.ds(SIDE * at_y, SIDE)
-        x = tok[0, four].reshape(256, 384)
-        y = jnp.dot(x, w[:, columns(n, 0)], preferred_element_type=F32).astype(BF16)
-        part[n, 0, four] = y.reshape(SIDE, 64, fh)
-        first_sends(n, 0, (at_y - yx[0] + SIDE) % SIDE)
-        y = jnp.dot(x, w[:, columns(n, 1)], preferred_element_type=F32).astype(BF16)
-        for at_x in range(SIDE):
-            part[n, 1, SIDE * at_x + at_y] = y[64 * at_x : 64 * at_x + 64]
-        role = (at_y - yx[0] + SIDE) % SIDE
-        right, left = grid_device(0, 1), grid_device(0, -1)
-        ssem = send.at[n, 1, 0]
-
-        @pl.when(role == 2)
-        def _():
-            for j in range(SIDE):
-                far = part.at[n, 1, slot(1, j, 2)]
-                push(far.at[lo], f1.at[n, 1, j, 0], ssem, f1_sem.at[n, 1, j, 0], right)
-                push(far.at[hi], f1.at[n, 1, j, 1], ssem, f1_sem.at[n, 1, j, 1], left)
-
-        @pl.when(role == 1)
-        def _():
-            for j in range(SIDE):
-                push(part.at[n, 1, slot(1, j, 1), hi], r1.at[n, 1, j, 0, hi], ssem, r1_sem.at[n, 1, j], right)
-
-        @pl.when(role == 3)
-        def _():
-            for j in range(SIDE):
-                push(part.at[n, 1, slot(1, j, 3), lo], r1.at[n, 1, j, 1, lo], ssem, r1_sem.at[n, 1, j], left)
+        task_i(n, 0, (waves[wave] - yx[0] + SIDE) % SIDE)
 
     def task_i(n, h, j):
         four = pl.ds(SIDE * group(h, j), SIDE)
         x = tok[h, four].reshape(256, 384)
-        y = jnp.dot(x, w[:, columns(n, h)], preferred_element_type=F32).astype(BF16)
-        part[n, h, four] = y.reshape(SIDE, 64, fh)
+        y = jnp.dot(x, w[:, summed(n, h)], preferred_element_type=F32).astype(BF16)
+        part[n][h][four] = y.reshape(SIDE, 64, y.shape[-1])
         first_sends(n, h, j)
 
     def forward(n, h, j, way):
         axis_a = ring(h)[0]
         device = grid_device(axis_a, 1 - 2 * way)
         rows, near = (lo, 1) if way == 0 else (hi, 3)
-        arrived(f1.at[n, h, j, way], f1_sem.at[n, h, j, way])
-        f1[n, h, j, way] = (
-            f1[n, h, j, way].astype(F32) + part[n, h, slot(h, j, near), rows].astype(F32)
+        arrived(f1[n][h].at[j, way], f1_sem.at[n, h, j, way])
+        f1[n][h][j, way] = (
+            f1[n][h][j, way].astype(F32) + part[n][h][slot(h, j, near), rows].astype(F32)
         ).astype(BF16)
-        push(f1.at[n, h, j, way], r1.at[n, h, j, way, rows], send.at[n, h, 1], r1_sem.at[n, h, j], device)
+        push(f1[n][h].at[j, way], r1[n][h].at[j, way, rows], send.at[n, h, 1], r1_sem.at[n, h, j], device)
 
     def task_f(n, h, j):
         forward(n, h, j, 0)
         forward(n, h, j, 1)
 
-    def task_fq(n, wave):
-        role = (waves[wave] - yx[0] + SIDE) % SIDE
-
-        @pl.when(role == 1)
-        def _():
-            for j in range(SIDE):
-                forward(n, 1, j, 0)
-
-        @pl.when(role == 3)
-        def _():
-            for j in range(SIDE):
-                forward(n, 1, j, 1)
-
     def sum_first(n, h, j):
-        arrived(r1.at[n, h, j], r1_sem.at[n, h, j])
-        total = part[n, h, slot(h, j, 0)].astype(F32)
-        total = total + r1[n, h, j, 0].astype(F32) + r1[n, h, j, 1].astype(F32)
-        s[n, h, j] = total.astype(BF16)
+        arrived(r1[n][h].at[j], r1_sem.at[n, h, j])
+        total = part[n][h][slot(h, j, 0)].astype(F32)
+        total = total + r1[n][h][j, 0].astype(F32) + r1[n][h][j, 1].astype(F32)
+        s[n][h][j] = total.astype(BF16)
 
     def second_sends(n, h, j):
         axis_b = ring(h)[1]
         right, left = grid_device(axis_b, 1), grid_device(axis_b, -1)
         ssem = send.at[n, h, 2]
         if j == 2:
-            push(s.at[n, h, 2, lo], f2.at[n, h, 0], ssem, f2_sem.at[n, h], right)
-            push(s.at[n, h, 2, hi], f2.at[n, h, 1], ssem, f2_sem.at[n, h], left)
+            push(s[n][h].at[2, lo], f2[n][h].at[0], ssem, f2_sem.at[n, h], right)
+            push(s[n][h].at[2, hi], f2[n][h].at[1], ssem, f2_sem.at[n, h], left)
         elif j == 1:
-            push(s.at[n, h, 1, hi], r2.at[n, h, 0, hi], ssem, r2_sem.at[n, h], right)
+            push(s[n][h].at[1, hi], r2[n][h].at[0, hi], ssem, r2_sem.at[n, h], right)
         elif j == 3:
-            push(s.at[n, h, 3, lo], r2.at[n, h, 1, lo], ssem, r2_sem.at[n, h], left)
+            push(s[n][h].at[3, lo], r2[n][h].at[1, lo], ssem, r2_sem.at[n, h], left)
 
     def task_d(n, h, j):
         sum_first(n, h, j)
@@ -256,24 +225,30 @@
         axis_b = ring(h)[1]
         right, left = grid_device(axis_b, 1), grid_device(axis_b, -1)
         ssem = send.at[n, h, 2]
-        arrived(f2.at[n, h], f2_sem.at[n, h])
-        f2[n, h, 0] = (f2[n, h, 0].astype(F32) + s[n, h, 1, lo].astype(F32)).astype(BF16)
-        push(f2.at[n, h, 0], r2.at[n, h, 0, lo], ssem, r2_sem.at[n, h], right)
-        f2[n, h, 1] = (f2[n, h, 1].astype(F32) + s[n, h, 3, hi].astype(F32)).astype(BF16)
-        push(f2.at[n, h, 1], r2.at[n, h, 1, hi], ssem, r2_sem.at[n, h], left)
+        arrived(f2[n][h], f2_sem.at[n, h])
+        f2[n][h][0] = (f2[n][h][0].astype(F32) + s[n][h][1, lo].astype(F32)).astype(BF16)
+        push(f2[n][h].at[0], r2[n][h].at[0, lo], ssem, r2_sem.at[n, h], right)
+        f2[n][h][1] = (f2[n][h][1].astype(F32) + s[n][h][3, hi].astype(F32)).astype(BF16)
+        push(f2[n][h].at[1], r2[n][h].at[1, hi], ssem, r2_sem.at[n, h], left)
 
     def task_d2(n, h):
-        arrived(r2.at[n, h], r2_sem.at[n, h])
-        mine = slot(h, 0, 0)
+        arrived(r2[n][h], r2_sem.at[n, h])
 
         @pl.loop(0, 4)
         def _(at):
             rows = pl.ds(pl.multiple_of(at * 16, 16), 16)
-            hidden = s[n, h, 0, rows].astype(F32) + r2[n, h, 0, rows].astype(F32) + r2[n, h, 1, rows].astype(F32)
+            hidden = s[n][h][0, rows].astype(F32) + r2[n][h][0, rows].astype(F32) + r2[n][h][1, rows].astype(F32)
             cdf, density = gelu_parts(hidden)
-            act[rows, columns(n, h)] = (hidden * cdf).astype(BF16)
-            grad = cot[rows, columns(n, h)].astype(F32) * (cdf + hidden * density)
-            g[n, h, mine, rows] = grad.astype(BF16)
+            act[rows, summed(n, h)] = (hidden * cdf).astype(BF16)
+            grad = cot[rows, summed(n, h)].astype(F32) * (cdf + hidden * density)
+            grad = grad.astype(BF16)
+            width = grad.shape[-1]
+            if h == 0:
+                g[n, 0, slot(0, 0, 0), rows, 0 : min(width, fh)] = grad[:, 0 : min(width, fh)]
+                if width > fh:
+                    g[n, 1, slot(1, 0, 0), rows, 0 : width - fh] = grad[:, fh:width]
+            else:
+                g[n, 1, slot(1, 0, 0), rows, fh - width : fh] = grad
 
     def block(c, h, j, i):
         n, start, size, _ = GATHERS[c]
@@ -320,6 +295,12 @@
         block_here(c, h, 2, 0)
         for delta in ways(c):
             share(c, h, 2, 0, axis_a, delta)
+
+    def task_a(c, h, step):
+        if step == 1:
+            task_a1(c, h)
+        else:
+            task_a2(c, h)
 
     def task_b(c, h, j):
         axis_a = ring(h)[0]
@@ -373,44 +354,41 @@
             term = jnp.dot(tok_t[h, t], rows, preferred_element_type=F32)
             total = term if total is None else total + term
         if start > 0:
-            total = gw[h] + total
+            total = gw[n, h] + total
         if start + size < 64:
-            gw[h] = total
+            gw[n, h] = total
         else:
             gwb[n, h] = total.astype(BF16)
             cols = columns(n, h)
             push(gwb.at[n, h], other_hbm.at[:, cols], dep_send.at[n, h], dep_recv.at[n, h], other)
             pltpu.make_async_copy(gwb.at[n, h], own_hbm.at[:, cols], out_sem.at[n, h]).start()
 
-    both = {"F": task_f, "D": task_d, "I": task_i, "B": task_b, "T": task_t}
-    both_once = {"F2": task_f2, "D2": task_d2, "S": task_s, "A1": task_a1, "A2": task_a2, "W": task_w}
+    by_half = {
+        "I": task_i, "F": task_f, "D": task_d, "G": task_f2, "H": task_d2,
+        "S": task_s, "A": task_a, "B": task_b, "T": task_t, "W": task_w,
+    }
+    without_step = "GHSW"
     cot_waited = False
-    for name, n, j in schedule():
-        if name == "D2" and not cot_waited:
+    for name, n, j in ORDER:
+        if name[0] == "H" and not cot_waited:
             loads[2].wait()
             cot_waited = True
-        if name in both:
-            for h in (0, 1):
-                both[name](n, h, j)
-        elif name in both_once:
-            for h in (0, 1):
-                both_once[name](n, h)
-        elif name == "Z":
+        if name == "Z":
             task_z(j)
         elif name == "IW":
             task_iw(n, j)
         elif name == "FP":
             task_f(n, 0, (waves[j] - yx[0] + SIDE) % SIDE)
-        elif name == "FQ":
-            task_fq(n, j)
         elif name == "DP":
             task_dp(n, j)
-        elif name == "DQ":
-            task_d(n, 1, j)
         elif name == "tokens":
             task_tokens()
         elif name == "transposes":
             task_transposes()
+        elif name[0] in without_step:
+            by_half[name[0]](n, int(name[1]))
+        else:
+            by_half[name[0]](n, int(name[1]), j)
 
     act_out = pltpu.make_async_copy(act, act_hbm, local_sem.at[0])
     act_out.start()
@@ -425,9 +403,9 @@
 
     for n in range(NCH):
         for h in (0, 1):
-            sent(r1.at[n, h], send.at[n, h, 0])
-            sent(s.at[n, h], send.at[n, h, 1])
-            sent(s.at[n, h, pl.ds(0, 3)], send.at[n, h, 2])
+            sent(r1[n][h], send.at[n, h, 0])
+            sent(s[n][h], send.at[n, h, 1])
+            sent(s[n][h].at[pl.ds(0, 3)], send.at[n, h, 2])
             cols = columns(n, h)
             pltpu.make_async_copy(gwb.at[n, h], own_hbm.at[:, cols], out_sem.at[n, h]).wait()
             done = remote(gwb.at[n, h], other_hbm.at[:, cols], dep_send.at[n, h], dep_recv.at[n, h], other)
@@ -452,6 +430,12 @@
     any_spec = pl.BlockSpec(memory_space=pl.ANY)
     vmem = pltpu.VMEM
     dma = pltpu.SemaphoreType.DMA
+
+    def halves(*shape):
+        return tuple(
+            tuple(vmem(shape + (2 * fh * part // 4,), BF16) for part in (share, 4 - share)) for share in X_FIRST
+        )
+
     act, own, other, gt = pl.pallas_call(
         kernel,
         out_shape=(
@@ -468,14 +452,14 @@
             vmem(cotangent.shape, BF16),
             vmem((2, 16, 64, d), BF16),
             vmem((2, 2, d, 512), BF16),
+            halves(16, 64),
+            halves(SIDE, 2, 32),
+            halves(SIDE, 2, 64),
+            halves(SIDE, 64),
+            halves(2, 32),
+            halves(2, 64),
             vmem((NCH, 2, 16, 64, fh), BF16),
-            vmem((NCH, 2, SIDE, 2, 32, fh), BF16),
-            vmem((NCH, 2, SIDE, 2, 64, fh), BF16),
-            vmem((NCH, 2, SIDE, 64, fh), BF16),
-            vmem((NCH, 2, 2, 32, fh), BF16),
-            vmem((NCH, 2, 2, 64, fh), BF16),
-            vmem((NCH, 2, 16, 64, fh), BF16),
-            vmem((2, d, fh), F32),
+            vmem((NCH, 2, d, fh), F32),
             vmem((NCH, 2, d, fh), BF16),
             vmem((16, 64, d), F32),
             vmem((16, 64, d), BF16),

time: 108 us -> 103 us (0.954)
  Pallas kernels: 102 us -> 95.8 us
    pallas_call x1, Pallas kernels: 102 us -> 95.8 us  [local(): pl.pallas_call(kernel, out_shape=(jax.ShapeDtypeStruct(cotangent.shape, B...]
where the time goes in v3:
time: 103 us; the launch traced here: 102 us
  Pallas kernels  95.8 us (93%)
  local copies, waits for them, and re-layouts  3.27 us (3%)
  other arithmetic  2.29 us (2%)
    pallas_call x1, Pallas kernels, local(): pl.pallas_call(kernel, out_shape=(jax.ShapeDtypeStruct(cotangent.shape, B...  95.8 us
    unnamed x6, local copies, waits for them, and re-layouts  3.27 us
    convert_element_type x1, other arithmetic, local(): grad_weight = (own.astype(F32) + other.astype(F32)).astype(BF16)  2.29 us

profile of v3, /device:TPU:4, one launch (start us, length us, event | category | flops | bytes accessed | tf_op | source)
XLA Modules:
  0.0 102.0 jit_solution(12691020444045623389)
XLA Ops:
  0.6 0.0 copy-start
  0.6 1.0 copy-done
  1.6 0.0 copy-start.1
  1.6 0.9 copy-done.1
  2.5 95.8 %shard_map.58 = (bf16[64,3072]{1,0:T(8,128)(2,1)S(1)}, bf16[384,3072]{1,0:T(8,128)(2,1)S(1)}, bf16[384,3072]{1,0:T(8,128)(2,1)S(1)}, bf16[2,64,384]{2,1,0:T(8,128)(2,1)S(1)}) custom-call(bf16[2,64,384]{2,1,0:T(8,128)(2,1)S(1)} %bitcast.2, bf16[384,3072]{1,0:T(8,128)(2,1)} %w_hbm.1, bf16[64,3072]{1,0:T(8,128)(2,1)S(1)} %copy-done), custom_call_target="tpu_custom_call" | custom-call | tf_op jit(solution)/shard_map/pallas_call | solution.py:439
  98.3 2.3 %add_convert_fusion = bf16[384,3072]{1,0:T(8,128)(2,1)} fusion(bf16[384,3072]{1,0:T(8,128)(2,1)S(1)} %get-tuple-element.10, bf16[384,3072]{1,0:T(8,128)(2,1)S(1)} %get-tuple-element.9), kind=kLoop, calls=%fused_computation | loop fusion | flops 4718592 | bytes 7077888 | tf_op jit(solution)/shard_map/convert_element_type | solution.py:487
  100.6 0.7 copy.8
  101.3 0.6 copy.9
Async XLA Ops:
  0.6 1.0 copy-start
  1.6 0.9 copy-start.1

commit v4 on v3

--- a/solution.py
+++ b/solution.py
@@ -10,7 +10,7 @@
 
 MESH = pl.DeviceIdType.MESH
 NCH = 2
-X_FIRST = (3, 2)
+X_FIRST = (8, 6)
 SIDE = 4
 ROWS = 8
 BF16 = jnp.bfloat16
@@ -28,21 +28,20 @@
 
 ORDER = (
     ("Z", 0, 1), ("IW", 0, 0), ("FP", 0, 0), ("Z", 0, 2), ("IW", 0, 1), ("DP", 0, 0), ("FP", 0, 1),
-    ("Z", 0, 3), ("Z", 0, 4), ("IW", 0, 2), ("IW", 0, 3), ("tokens", 0, 0), ("I1", 0, 0), ("I1", 0, 1),
-    ("I1", 0, 2), ("I1", 0, 3), ("DP", 0, 1), ("I0", 1, 0), ("I0", 1, 1), ("I0", 1, 2), ("I0", 1, 3),
-    ("FP", 0, 2), ("F1", 0, 0), ("I1", 1, 0), ("I1", 1, 1), ("F1", 0, 1), ("I1", 1, 2), ("I1", 1, 3),
-    ("F1", 0, 2), ("transposes", 0, 0), ("FP", 0, 3), ("F1", 0, 3), ("D1", 0, 0), ("F0", 1, 0), ("F1", 1, 0),
-    ("F0", 1, 1), ("F1", 1, 1), ("F0", 1, 2), ("D1", 0, 1), ("F1", 1, 2), ("F0", 1, 3), ("F1", 1, 3),
-    ("DP", 0, 2), ("D1", 0, 2), ("D1", 0, 3), ("DP", 0, 3), ("D1", 1, 0), ("D0", 1, 0), ("D1", 1, 1),
-    ("D0", 1, 1), ("D1", 1, 2), ("D0", 1, 2), ("D1", 1, 3), ("D0", 1, 3), ("G0", 0, 0), ("G1", 0, 0),
-    ("G0", 1, 0), ("G1", 1, 0), ("H1", 0, 0), ("H0", 0, 0), ("S0", 0, 0), ("S1", 0, 0), ("H0", 1, 0),
-    ("H1", 1, 0), ("S0", 1, 0), ("S1", 1, 0), ("A0", 0, 1), ("B0", 0, 0), ("B1", 0, 0), ("A1", 0, 1),
-    ("A0", 1, 1), ("B0", 1, 0), ("B1", 1, 0), ("A1", 1, 1), ("A0", 0, 2), ("T0", 0, 0), ("T1", 0, 0),
-    ("B0", 0, 3), ("B1", 0, 3), ("B0", 0, 1), ("B1", 0, 1), ("A1", 0, 2), ("A0", 1, 2), ("T0", 1, 0),
-    ("T1", 1, 0), ("B0", 1, 3), ("B1", 1, 3), ("B0", 1, 1), ("B1", 1, 1), ("A1", 1, 2), ("T1", 0, 3),
-    ("T1", 0, 1), ("B0", 0, 2), ("T0", 0, 1), ("T0", 0, 3), ("B1", 0, 2), ("T1", 1, 3), ("T1", 1, 1),
-    ("B0", 1, 2), ("T0", 1, 1), ("T0", 1, 3), ("B1", 1, 2), ("T1", 0, 2), ("T0", 0, 2), ("W0", 0, 0),
-    ("T0", 1, 2), ("T1", 1, 2), ("W1", 0, 0), ("W0", 1, 0), ("W1", 1, 0),
+    ("Z", 0, 3), ("Z", 0, 4), ("IW", 0, 2), ("IW", 0, 3), ("FQ", 0, 1), ("tokens", 0, 0), ("DP", 0, 1),
+    ("I0", 1, 0), ("I0", 1, 1), ("I0", 1, 2), ("FP", 0, 2), ("I0", 1, 3), ("I1", 1, 0), ("I1", 1, 1),
+    ("I1", 1, 2), ("I1", 1, 3), ("transposes", 0, 0), ("FP", 0, 3), ("FQ", 0, 0), ("F0", 1, 0), ("F1", 1, 0),
+    ("F0", 1, 1), ("F1", 1, 1), ("F0", 1, 2), ("F1", 1, 2), ("D1", 0, 0), ("DP", 0, 2), ("D1", 0, 1),
+    ("F0", 1, 3), ("D1", 0, 2), ("F1", 1, 3), ("D1", 0, 3), ("D1", 1, 0), ("DP", 0, 3), ("D1", 1, 1),
+    ("D0", 1, 0), ("D1", 1, 2), ("D0", 1, 1), ("D0", 1, 2), ("D1", 1, 3), ("D0", 1, 3), ("G0", 0, 0),
+    ("G1", 0, 0), ("G0", 1, 0), ("G1", 1, 0), ("H1", 0, 0), ("H0", 0, 0), ("S0", 0, 0), ("S1", 0, 0),
+    ("H0", 1, 0), ("H1", 1, 0), ("S0", 1, 0), ("S1", 1, 0), ("A0", 0, 1), ("B0", 0, 0), ("B1", 0, 0),
+    ("A1", 0, 1), ("A0", 1, 1), ("B0", 1, 0), ("B1", 1, 0), ("A1", 1, 1), ("A0", 0, 2), ("T0", 0, 0),
+    ("T1", 0, 0), ("B0", 0, 3), ("B1", 0, 3), ("B0", 0, 1), ("B1", 0, 1), ("A1", 0, 2), ("A0", 1, 2),
+    ("T0", 1, 0), ("T1", 1, 0), ("B0", 1, 3), ("B1", 1, 3), ("B0", 1, 1), ("B1", 1, 1), ("A1", 1, 2),
+    ("T1", 0, 3), ("T1", 0, 1), ("B0", 0, 2), ("T0", 0, 1), ("T0", 0, 3), ("B1", 0, 2), ("T1", 1, 3),
+    ("T1", 1, 1), ("B0", 1, 2), ("T0", 1, 1), ("T0", 1, 3), ("B1", 1, 2), ("T1", 0, 2), ("T0", 0, 2),
+    ("W0", 0, 0), ("T0", 1, 2), ("T1", 1, 2), ("W1", 0, 0), ("W0", 1, 0), ("W1", 1, 0),
 )
 
 
@@ -170,7 +169,32 @@
     def task_iw(n, wave):
         if wave == 0:
             loads[1].wait()
-        task_i(n, 0, (waves[wave] - yx[0] + SIDE) % SIDE)
+        at_y = waves[wave]
+        role = (at_y - yx[0] + SIDE) % SIDE
+        task_i(n, 0, role)
+        x = tok[0, pl.ds(SIDE * at_y, SIDE)].reshape(256, 384)
+        y = jnp.dot(x, w[:, summed(n, 1)], preferred_element_type=F32).astype(BF16)
+        for at_x in range(SIDE):
+            part[n][1][SIDE * at_x + at_y] = y[64 * at_x : 64 * at_x + 64]
+        right, left = grid_device(0, 1), grid_device(0, -1)
+        ssem = send.at[n, 1, 0]
+
+        @pl.when(role == 2)
+        def _():
+            for j in range(SIDE):
+                far = part[n][1].at[slot(1, j, 2)]
+                push(far.at[lo], f1[n][1].at[j, 0], ssem, f1_sem.at[n, 1, j, 0], right)
+                push(far.at[hi], f1[n][1].at[j, 1], ssem, f1_sem.at[n, 1, j, 1], left)
+
+        @pl.when(role == 1)
+        def _():
+            for j in range(SIDE):
+                push(part[n][1].at[slot(1, j, 1), hi], r1[n][1].at[j, 0, hi], ssem, r1_sem.at[n, 1, j], right)
+
+        @pl.when(role == 3)
+        def _():
+            for j in range(SIDE):
+                push(part[n][1].at[slot(1, j, 3), lo], r1[n][1].at[j, 1, lo], ssem, r1_sem.at[n, 1, j], left)
 
     def task_i(n, h, j):
         four = pl.ds(SIDE * group(h, j), SIDE)
@@ -379,6 +403,9 @@
             task_iw(n, j)
         elif name == "FP":
             task_f(n, 0, (waves[j] - yx[0] + SIDE) % SIDE)
+        elif name == "FQ":
+            for k in range(SIDE):
+                forward(n, 1, k, j)
         elif name == "DP":
             task_dp(n, j)
         elif name == "tokens":
@@ -424,6 +451,20 @@
     gt_out.wait()
 
 
+def finish(own, other, act, gt, gw_out, act_out, gt_out, total, sem):
+    copies = [pltpu.make_async_copy(act, act_out, sem.at[6]), pltpu.make_async_copy(gt, gt_out, sem.at[7])]
+    for copy in copies:
+        copy.start()
+    step = own.shape[0] // 6
+    for k in range(6):
+        rows = pl.ds(k * step, step)
+        total[rows] = (own[rows].astype(F32) + other[rows].astype(F32)).astype(BF16)
+        copies.append(pltpu.make_async_copy(total.at[rows], gw_out.at[rows], sem.at[k]))
+        copies[-1].start()
+    for copy in copies:
+        copy.wait()
+
+
 def local(tokens, weight, cotangent):
     d, f = weight.shape
     fh = f // (2 * NCH)
@@ -433,7 +474,7 @@
 
     def halves(*shape):
         return tuple(
-            tuple(vmem(shape + (2 * fh * part // 4,), BF16) for part in (share, 4 - share)) for share in X_FIRST
+            tuple(vmem(shape + (2 * fh * part // 12,), BF16) for part in (share, 12 - share)) for share in X_FIRST
         )
 
     act, own, other, gt = pl.pallas_call(
@@ -484,7 +525,18 @@
             collective_id=0, has_side_effects=True, vmem_limit_bytes=48 * 2**20
         ),
     )(tokens.reshape(2, 64, d), weight, cotangent)
-    grad_weight = (own.astype(F32) + other.astype(F32)).astype(BF16)
+    grad_weight, act, gt = pl.pallas_call(
+        finish,
+        out_shape=(
+            jax.ShapeDtypeStruct(weight.shape, BF16),
+            jax.ShapeDtypeStruct(cotangent.shape, BF16),
+            jax.ShapeDtypeStruct((2, 64, d), BF16),
+        ),
+        in_specs=[pl.BlockSpec(memory_space=vmem)] * 4,
+        out_specs=(pl.BlockSpec(memory_space=pltpu.HBM),) * 3,
+        scratch_shapes=[vmem(weight.shape, BF16), dma((8,))],
+        compiler_params=pltpu.CompilerParams(vmem_limit_bytes=8 * 2**20),
+    )(own, other, act, gt)
     return (act, gt.reshape(128, d), grad_weight)
 
 

time: 103 us -> 100 us (0.971); the launches traced: 102 us -> 100 us
  other arithmetic: 2.29 us -> 0 us
  Pallas kernels: 95.8 us -> 97.6 us
  local copies, waits for them, and re-layouts: 3.27 us -> 1.88 us
    convert_element_type x1 -> x0, other arithmetic: 2.29 us -> none  [local(): grad_weight = (own.astype(F32) + other.astype(F32)).astype(BF16)]
    pallas_call x0 -> x1, Pallas kernels: none -> 1.63 us  [local(): pl.pallas_call(finish, out_shape=(jax.ShapeDtypeStruct(weight.shape, BF16...]
    unnamed x6 -> x4, local copies, waits for them, and re-layouts: 3.27 us -> 1.88 us
where the time goes in v4:
time: 100 us
  Pallas kernels  97.6 us (98%)
  local copies, waits for them, and re-layouts  1.88 us (2%)
    pallas_call x1, Pallas kernels, local(): pl.pallas_call(kernel, out_shape=(jax.ShapeDtypeStruct(cotangent.shape, B...  96 us

profile of v4, /device:TPU:4, one launch (start us, length us, event | category | flops | bytes accessed | tf_op | source)
XLA Modules:
  0.0 100.3 jit_solution(9807976835320009880)
XLA Ops:
  0.6 0.0 copy-start
  0.6 1.0 copy-done
  1.6 0.0 copy-start.1
  1.6 0.9 copy-done.1
  2.5 96.0 %shard_map.58 = (bf16[64,3072]{1,0:T(8,128)(2,1)S(1)}, bf16[384,3072]{1,0:T(8,128)(2,1)S(1)}, bf16[384,3072]{1,0:T(8,128)(2,1)S(1)}, bf16[2,64,384]{2,1,0:T(8,128)(2,1)S(1)}) custom-call(bf16[2,64,384]{2,1,0:T(8,128)(2,1)S(1)} %bitcast.2, bf16[384,3072]{1,0:T(8,128)(2,1)} %w_hbm.1, bf16[64,3072]{1,0:T(8,128)(2,1)S(1)} %copy-done), custom_call_target="tpu_custom_call" | custom-call | tf_op jit(solution)/shard_map/pallas_call | solution.py:480
  98.5 1.6 %shard_map.59 = (bf16[384,3072]{1,0:T(8,128)(2,1)}, bf16[64,3072]{1,0:T(8,128)(2,1)}, bf16[2,64,384]{2,1,0:T(8,128)(2,1)}) custom-call(bf16[384,3072]{1,0:T(8,128)(2,1)S(1)} %get-tuple-element.10.own, bf16[384,3072]{1,0:T(8,128)(2,1)S(1)} %get-tuple-element.11.other, bf16[64,3072]{1,0:T(8,128)(2,1)S(1)} %get-tuple-element.12.act, ...), custom_call_target="tpu_custom_call" | custom-call | tf_op jit(solution)/shard_map/pallas_call | solution.py:528
Async XLA Ops:
  0.6 1.0 copy-start
  1.6 0.9 copy-start.1

commit v5 on v4

--- a/solution.py
+++ b/solution.py
@@ -392,6 +392,8 @@
         "S": task_s, "A": task_a, "B": task_b, "T": task_t, "W": task_w,
     }
     without_step = "GHSW"
+    act_out = pltpu.make_async_copy(act, act_hbm, local_sem.at[0])
+    halves_done = 0
     cot_waited = False
     for name, n, j in ORDER:
         if name[0] == "H" and not cot_waited:
@@ -414,11 +416,25 @@
             task_transposes()
         elif name[0] in without_step:
             by_half[name[0]](n, int(name[1]))
+            halves_done += name[0] == "H"
+            if name[0] == "H" and halves_done == 2 * NCH:
+                act_out.start()
         else:
             by_half[name[0]](n, int(name[1]), j)
 
-    act_out = pltpu.make_async_copy(act, act_hbm, local_sem.at[0])
-    act_out.start()
+    for n in range(NCH):
+        for h in (0, 1):
+            sent(r1[n][h], send.at[n, h, 0])
+            sent(s[n][h], send.at[n, h, 1])
+            sent(s[n][h].at[pl.ds(0, 3)], send.at[n, h, 2])
+    for c, (n, start, size, _) in enumerate(GATHERS):
+        for h in (0, 1):
+            sent(g.at[n, h, pl.ds(0, 15), pl.ds(start, size)], g_send.at[c, h])
+    for delta in range(4):
+        for k in (0, 1):
+            for way in (0, 1):
+                if delta < 3 or k == way:
+                    sent(tok.at[0, 0], z_send.at[4 * delta + 2 * k + way])
     arrived(zrecv, zs_recv.at[0])
     for at in range(2):
         total = gt[2 * row + at].astype(BF16).astype(F32)
@@ -430,22 +446,11 @@
 
     for n in range(NCH):
         for h in (0, 1):
-            sent(r1[n][h], send.at[n, h, 0])
-            sent(s[n][h], send.at[n, h, 1])
-            sent(s[n][h].at[pl.ds(0, 3)], send.at[n, h, 2])
             cols = columns(n, h)
             pltpu.make_async_copy(gwb.at[n, h], own_hbm.at[:, cols], out_sem.at[n, h]).wait()
             done = remote(gwb.at[n, h], other_hbm.at[:, cols], dep_send.at[n, h], dep_recv.at[n, h], other)
             done.wait_send()
             done.wait_recv()
-    for c, (n, start, size, _) in enumerate(GATHERS):
-        for h in (0, 1):
-            sent(g.at[n, h, pl.ds(0, 15), pl.ds(start, size)], g_send.at[c, h])
-    for delta in range(4):
-        for k in (0, 1):
-            for way in (0, 1):
-                if delta < 3 or k == way:
-                    sent(tok.at[0, 0], z_send.at[4 * delta + 2 * k + way])
     sent(zsend.at[pl.ds(0, 14)], zs_send.at[0])
     act_out.wait()
     gt_out.wait()

time: 100 us -> 100 us (level)
  no operation moved by 1% of the time
where the time goes in v5:
time: 100 us
  Pallas kernels  97.6 us (98%)
  local copies, waits for them, and re-layouts  1.88 us (2%)
    pallas_call x1, Pallas kernels, local(): pl.pallas_call(kernel, out_shape=(jax.ShapeDtypeStruct(cotangent.shape, B...  95.9 us

profile of v5, /device:TPU:4, one launch (start us, length us, event | category | flops | bytes accessed | tf_op | source)
XLA Modules:
  0.0 100.3 jit_solution(2963813713035163743)
XLA Ops:
  0.6 0.0 copy-start
  0.6 1.0 copy-done
  1.6 0.0 copy-start.1
  1.6 0.9 copy-done.1
  2.5 95.9 %shard_map.58 = (bf16[64,3072]{1,0:T(8,128)(2,1)S(1)}, bf16[384,3072]{1,0:T(8,128)(2,1)S(1)}, bf16[384,3072]{1,0:T(8,128)(2,1)S(1)}, bf16[2,64,384]{2,1,0:T(8,128)(2,1)S(1)}) custom-call(bf16[2,64,384]{2,1,0:T(8,128)(2,1)S(1)} %bitcast.2, bf16[384,3072]{1,0:T(8,128)(2,1)} %w_hbm.1, bf16[64,3072]{1,0:T(8,128)(2,1)S(1)} %copy-done), custom_call_target="tpu_custom_call" | custom-call | tf_op jit(solution)/shard_map/pallas_call | solution.py:485
  98.5 1.6 %shard_map.59 = (bf16[384,3072]{1,0:T(8,128)(2,1)}, bf16[64,3072]{1,0:T(8,128)(2,1)}, bf16[2,64,384]{2,1,0:T(8,128)(2,1)}) custom-call(bf16[384,3072]{1,0:T(8,128)(2,1)S(1)} %get-tuple-element.10.own, bf16[384,3072]{1,0:T(8,128)(2,1)S(1)} %get-tuple-element.11.other, bf16[64,3072]{1,0:T(8,128)(2,1)S(1)} %get-tuple-element.12.act, ...), custom_call_target="tpu_custom_call" | custom-call | tf_op jit(solution)/shard_map/pallas_call | solution.py:533
Async XLA Ops:
  0.6 1.0 copy-start
  1.6 0.9 copy-start.1
